TPU v7x, 32 devices: a whole 2x2x4 slice. The times are simulated.
32 devices in a mesh: row: 4 (over z), col: 8 (over y, x, core).
Axes of the slice: x: 2, y: 2, z: 4, core: 2. Of those that a mesh axis runs over, the one named last changes fastest.
Arguments:
- points: float32 [4, 4, 262144], P(None, None, ('row', 'col')), may hold values from -0.4 to 1.4, as said below
- density: float32 [262144], P(('row', 'col')), may hold values from -6 to 6
- near_pairs: int32 [192, 2], P(('row', 'col')), may hold values from 0 to 127, as said below
- far_pairs: int32 [512, 2], P(('row', 'col')), may hold values from 0 to 127, as said below
- near_count: int32 [32], P(('row', 'col')), may hold values from 1 to 6
- far_count: int32 [32], P(('row', 'col')), may hold values from 1 to 16
Outputs:
- potential: float32 [262144], P(('row', 'col'))
Inputs may be any that keep to these rules, and one draw needn't show every extreme that they name: `near_pairs`: the first column indexes target band blocks and the second source band blocks (below 64). On device (r, c) the first column lies in c * 16 to c * 16 + 15, so every near target block is one of the device's own blocks. The first slot of each device names one of its own blocks k as (c * 16 + k, r * 16 + k). `far_pairs`: the first column indexes target band blocks (below 128), the second source band blocks (below 64). `points`: weights (entry 3) lie in 0.01 to 0.04; coordinates in -0.4 to 1.4.
All inputs are finite; a program needn't handle non-finite values.
Results may differ from a plain program's by a relative error of at most 0.0003.
Values sent between devices are 32-bit elements; how exact they have to be, the bound alone decides.
No kernel may reach another device: no remote copies, remote signals or barrier semaphores. Data moves between devices by JAX's collectives and lax.ppermute only.
A program may use at most 64 MiB of HBM per device.

v0:
```python
import functools

import jax
import jax.numpy as jnp
from jax import lax
from jax.experimental import pallas as pl
from jax.experimental.pallas import tpu as pltpu
from jax.sharding import PartitionSpec as P

BLK = 512
LANES = 128
SOFT_SQ = 0.0004
TERMS = 64
SPLIT = 48
HALF = 512
QUARTERS = 4
SLOTS = 5
NEAR_SCRATCH = 4 * [None]
GROUP = 16
CHUNK = 512
VMEM = pl.BlockSpec(memory_space=pltpu.VMEM)
SMEM = pl.BlockSpec(memory_space=pltpu.SMEM)
ANY = pl.BlockSpec(memory_space=pl.ANY)
HBM = pl.BlockSpec(memory_space=pltpu.HBM)
PARAMS = pltpu.CompilerParams(vmem_limit_bytes=40 * 1024 * 1024)


def prep_kernel(near_hbm, count, far_hbm, pts_hbm, dens_hbm, msg, far_out, near_out, weight_out, *scratch):
    near_ref, far_ref, pts_ref, dens_ref, sems = scratch
    blocks = near_out.shape[0]
    quad = pts_ref.shape[1]
    slots, body = near_ref.shape[1] - 1, quad * 4
    base = near_lines(slots, quad)
    width = pts_ref.shape[2] // QUARTERS
    copies = [
        pltpu.make_async_copy(dens_hbm, dens_ref, sems.at[QUARTERS]),
        pltpu.make_async_copy(far_hbm, far_ref, sems.at[QUARTERS + 1]),
        pltpu.make_async_copy(near_hbm, near_ref, sems.at[QUARTERS + 2]),
    ]
    for i in range(QUARTERS):
        part = slice(i * width, (i + 1) * width)
        copies.append(pltpu.make_async_copy(pts_hbm.at[:, :, part], pts_ref.at[:, :, part], sems.at[i]))
    for copy in copies:
        copy.start()
    copies.pop(0).wait()
    copies.pop(0).wait()
    copies.pop(0).wait()

    def put_far(k, value):
        far_out[k] = value
        msg[base + 4 * k : base + 4 * k + 4, :] = value

    for k in range(blocks):
        cols = slice(k * BLK, (k + 1) * BLK)
        if k % (blocks // QUARTERS) == 0:
            copies.pop(0).wait()
        w = pts_ref[3, :, cols]
        total = jnp.sum(w, axis=0, keepdims=True)
        dens = jnp.concatenate([dens_ref[4 * k + q : 4 * k + q + 1, :] for q in range(4)], axis=1)
        lines = []
        for c in range(3):
            x = pts_ref[c, :, cols]
            lines.append(jnp.sum(x * w, axis=0, keepdims=True) / total)
            near_out[k, quad * c : quad * c + quad, :] = x
        near_out[k, quad * 3 : quad * 4, :] = w
        near_out[k, quad * 4 : quad * 4 + 8, :] = jnp.broadcast_to(dens, (8, BLK))
        put_far(k, jnp.concatenate(lines + [total * dens], axis=0))
        weight_out[k : k + 1, :] = total
    lane = lax.broadcasted_iota(jnp.int32, (1, LANES), 1)
    lines = [jnp.full((1, LANES), -1.0, jnp.float32)] * 2
    for t in range(slots):
        k = lax.rem(near_ref[0, t + 1], blocks)
        msg[t * body : (t + 1) * body, :] = near_out[k, 0:body, :]
        source = jnp.where(t + 1 < count[0], near_ref[1, t + 1], -1)
        lines[0] = jnp.where(lane == t, k.astype(jnp.float32), lines[0])
        lines[1] = jnp.where(lane == t, source.astype(jnp.float32), lines[1])
    pairs = jnp.concatenate([far_ref[...].astype(jnp.float32), jnp.full((2, LANES - far_ref.shape[1]), -1.0)], axis=1)
    pairs = jnp.concatenate([pairs] + lines, axis=0)
    put_far(blocks, jnp.concatenate([pairs] * (BLK // LANES), axis=1))
    used = base + 4 * (blocks + 1)
    if used < msg.shape[0]:
        msg[used:, :] = jnp.zeros((msg.shape[0] - used, BLK), jnp.float32)


def near_lines(slots, quad):
    return slots * 4 * quad


def three(value):
    one = value.astype(jnp.bfloat16).astype(jnp.float32)
    two = (value - one).astype(jnp.bfloat16).astype(jnp.float32)
    return one, two, value - one - two


def pick_row(row, values):
    out = jnp.zeros(row.shape, jnp.float32)
    for k, value in enumerate(values):
        out = jnp.where(row == k, value, out)
    return out


def parts(x):
    row = lax.broadcasted_iota(jnp.int32, x.shape, 0)
    live = row < 3
    centred = jnp.where(live, x - 0.5, 0.0)
    head = jnp.round(centred * 256.0) * (1.0 / 256.0)
    rest = centred - head
    rest1 = rest.astype(jnp.bfloat16).astype(jnp.float32)
    big = pick_row(row, three(jnp.sum(head * head, axis=0, keepdims=True)))
    small = pick_row(row, three(jnp.sum(rest * (2.0 * head + rest), axis=0, keepdims=True) + 0.5 * SOFT_SQ))
    return head, rest1, rest - rest1, big, small, jnp.where(live, 1.0, 0.0)


def left_terms(x, columns):
    head, rest1, rest2, big, small, ones = parts(x)
    h2, a2, b2 = -2.0 * head, -2.0 * rest1, -2.0 * rest2
    groups = [h2, big, ones, small, ones, h2, h2, a2, b2, a2, a2, b2]
    row = lax.broadcasted_iota(jnp.int32, (TERMS - SPLIT, x.shape[1]), 0)
    groups.append(pick_row(row, [part for column in columns for part in three(column)]))
    return jnp.concatenate(groups, axis=0)


def right_terms(x):
    head, rest1, rest2, big, small, ones = parts(x)
    groups = [head, ones, big, ones, small, rest1, rest2, head, head, rest1, rest2, rest1]
    groups.append(jnp.zeros((TERMS - SPLIT, x.shape[1]), jnp.float32))
    return jnp.concatenate(groups, axis=0).astype(jnp.bfloat16)


def column_of(lhs, which):
    row = lax.broadcasted_iota(jnp.int32, (TERMS, LANES), 0) - SPLIT - 3 * which
    pick = jnp.where((row >= 0) & (row < 3), 1.0, 0.0).astype(jnp.bfloat16)
    return jnp.dot(lhs, pick, preferred_element_type=jnp.float32)


def fold_lanes(tile, row):
    part = tile[:, :LANES] * row[:, :LANES]
    for q in range(1, tile.shape[1] // LANES):
        part = part + tile[:, q * LANES : (q + 1) * LANES] * row[:, q * LANES : (q + 1) * LANES]
    return part


def twice(col):
    return jnp.concatenate([col] * (HALF // LANES), axis=1)


def place(x, n):
    bits = n.bit_length() - 1
    div, rem = (lambda a, b: a // b, lambda a, b: a % b) if isinstance(x, int) else (lax.div, lax.rem)
    return sum(rem(div(x, 1 << (bits - 1 - j)), 2) * (1 << j) for j in range(bits))


def far_tiles(pairs, count, row_in, sources, rows_out, cols_out, base, queue, left_buf, right_buf, lhs_buf, rhs_buf, part_buf):
    n_col = lax.axis_size("col")
    row_step = 2 * row_in[0].shape[0] // n_col
    blocks = row_step - 1
    my_row, my_col = lax.axis_index("row"), lax.axis_index("col")

    def ways(s):
        a, b = pairs[0, s], pairs[1, s]
        return jnp.bitwise_xor(lax.div(a, blocks), my_col), jnp.bitwise_xor(lax.div(b, blocks), my_row)

    def enqueue(s, n):
        b_way = ways(s)[1]
        here = functools.reduce(jnp.logical_or, [b_way == d for d in sources])

        @pl.when(here)
        def _():
            queue[n] = s

        return n + here.astype(jnp.int32)

    def fetch(s, j):
        a_way, b_way = ways(s)
        ka, kb = lax.rem(pairs[0, s], blocks), lax.rem(pairs[1, s], blocks)
        for d, other in sources.items():

            @pl.when(b_way == d)
            def _():
                if d == 0:
                    right_buf[j] = other[kb]
                else:
                    lines = [other[pl.ds(base + 4 * kb + c, 1), :] for c in range(4)]
                    right_buf[j] = jnp.concatenate(lines, axis=0)

        for core, half in enumerate(row_in):

            @pl.when(lax.rem(a_way, 2) == core)
            def _():
                left_buf[j] = half[place(lax.div(a_way, 2), n_col // 2) * row_step + ka]

        return jnp.where((a_way == 0) & (b_way == 0) & (ka == kb), 0.0, 1.0)

    def tiles(slots):
        many = range(len(slots))
        mirror = [fetch(s, j) for j, s in enumerate(slots)]
        for j in many:
            left = left_buf[j]
            lhs_buf[j] = jnp.transpose(left_terms(left, [left[3:4]])).astype(jnp.bfloat16)
            rhs_buf[j] = right_terms(right_buf[j])
        zcol = [column_of(lhs_buf[j], 0) for j in many]
        dist = [jnp.dot(lhs_buf[j], rhs_buf[j], preferred_element_type=jnp.float32) for j in many]
        weights = [right_buf[j, 3:4, :] for j in many]
        acc = [jnp.zeros((8, BLK), jnp.float32) for _ in many]
        for g in range(BLK // 8):
            rows = slice(g * 8, (g + 1) * 8)
            for j in many:
                tile = lax.rsqrt(dist[j][rows, :])
                part_buf[j, rows, :] = fold_lanes(tile, weights[j])
                acc[j] = acc[j] + tile * twice(zcol[j][rows, :])
        for j, s in enumerate(slots):
            rows_out[pl.ds(s, 1), :] = jnp.sum(jnp.transpose(part_buf[j]), axis=0, keepdims=True)
            cols_out[pl.ds(s, 1), :] = jnp.sum(acc[j], axis=0, keepdims=True) * mirror[j]

    def two(i, _):
        tiles([queue[2 * i], queue[2 * i + 1]])
        return 0

    total = lax.fori_loop(0, count[0], enqueue, 0)
    lax.fori_loop(0, lax.div(total, 2), two, 0)
    pl.when(lax.rem(total, 2) == 1)(lambda: tiles([queue[total - 1]]))


def points(tall):
    quad = tall.shape[0] // 4
    sides = [[tall[quad * c + u : quad * c + u + 1, :] for c in range(4)] for u in range(quad)]
    return jnp.concatenate([jnp.concatenate(side, axis=0) for side in sides], axis=1)


def near_tile(left, dens_i, right, dens_j, lhs_buf, rhs_buf, part_buf, acc_buf):
    quad = left.shape[1] // BLK
    terms = jnp.transpose(left_terms(left, [left[3:4], jnp.concatenate([dens_i] * quad, axis=1)]))
    terms = terms.astype(jnp.bfloat16)
    for g in range(BLK // GROUP):
        for u in range(quad):
            to, at = (g * quad + u) * GROUP, u * BLK + g * GROUP
            lhs_buf[to : to + GROUP, :] = terms[at : at + GROUP, :]
    rhs_buf[...] = right_terms(right)
    weights = right[3:4]
    acc_buf[...] = jnp.zeros_like(acc_buf)

    def chunk(i, _):
        at = pl.multiple_of(i * CHUNK * quad, CHUNK * quad)
        lhs = lhs_buf[pl.ds(at, CHUNK * quad), :]
        wcol = column_of(lhs, 0)
        groups = CHUNK // GROUP
        first_rows = [lhs[g * quad * GROUP : g * quad * GROUP + GROUP, :] for g in range(groups)]
        dcol = column_of(jnp.concatenate(first_rows, axis=0), 1)
        part = None
        for h in range(BLK // HALF):
            tiles = [None] * groups
            for v in range(quad):
                cols = slice(v * BLK + h * HALF, v * BLK + (h + 1) * HALF)
                dist = jnp.dot(lhs, rhs_buf[:, cols], preferred_element_type=jnp.float32)
                for g in range(groups):
                    inner = None
                    for u in range(quad):
                        rows = slice((g * quad + u) * GROUP, (g * quad + u + 1) * GROUP)
                        term = lax.rsqrt(dist[rows, :]) * twice(wcol[rows, :])
                        inner = term if inner is None else inner + term
                    inner = inner * weights[:, cols]
                    tiles[g] = inner if tiles[g] is None else tiles[g] + inner
            tile = jnp.concatenate(tiles, axis=0)
            cols = slice(h * HALF, (h + 1) * HALF)
            more = fold_lanes(tile, dens_j[:, cols])
            part = more if part is None else part + more
            acc_buf[:, cols] += jnp.sum((tile * twice(dcol)).reshape(-1, 8, HALF), axis=0)
        part_buf[pl.ds(pl.multiple_of(i * CHUNK, CHUNK), CHUNK), :] = part
        return 0

    lax.fori_loop(0, BLK // CHUNK, chunk, 0)
    rows = jnp.sum(jnp.transpose(part_buf[...]), axis=0, keepdims=True)
    return rows, jnp.sum(acc_buf[...], axis=0, keepdims=True)


def near_own_kernel(pairs, count, near_ref, field, *bufs):
    blocks, depth, _ = near_ref.shape
    body = depth - 8
    my_row = lax.axis_index("row")
    field[...] = jnp.zeros_like(field)

    def step(s, _):
        ka, kb = lax.rem(pairs[0, s], blocks), pairs[1, s] - my_row * blocks

        @pl.when((kb >= 0) & (kb < blocks))
        def _():
            left, right = points(near_ref[ka, 0:body, :]), points(near_ref[kb, 0:body, :])
            dens_i, dens_j = near_ref[ka, body : body + 1, :], near_ref[kb, body : body + 1, :]
            rows, cols = near_tile(left, dens_i, right, dens_j, *bufs)
            field[pl.ds(ka, 1), :] += rows
            field[pl.ds(kb, 1), :] += cols * jnp.where(ka == kb, 0.0, 1.0)

        return 0

    lax.fori_loop(0, count[0], step, 0)


def near_tiles(meanwhile, near_ref, got, field, put, right_buf, tags, sems, *bufs):
    blocks, depth, _ = near_ref.shape
    body = depth - 8
    base = near_lines(SLOTS, body // 4)
    my_row = lax.axis_index("row")
    tail = slice(base + 4 * blocks, base + 4 * blocks + 8)
    copies = [pltpu.make_async_copy(g.at[tail, 0:LANES], tags.at[d], sems.at[d]) for d, g in enumerate(got)]
    for copy in copies:
        copy.start()
    meanwhile()
    for copy in copies:
        copy.wait()

    def step(i, _):
        way, t = lax.div(i, SLOTS), lax.rem(i, SLOTS)
        kb = tags[way, 3, t].astype(jnp.int32) - my_row * blocks

        @pl.when((kb >= 0) & (kb < blocks))
        def _():
            for d, other in enumerate(got):

                @pl.when(way == d)
                def _():
                    at = pl.multiple_of(t * body, 8)
                    points_j = other[pl.ds(at, body), :]
                    line = base + 4 * tags[way, 2, t].astype(jnp.int32) + 3
                    total = jnp.sum(points_j[body - body // 4 :], axis=0, keepdims=True)
                    right_buf[0:body, :] = points_j
                    right_buf[body : body + 1, :] = other[pl.ds(line, 1), :] / total

            left, right = points(near_ref[kb, 0:body, :]), points(right_buf[0:body, :])
            dens_i, dens_j = near_ref[kb, body : body + 1, :], right_buf[body : body + 1, :]
            rows, cols = near_tile(left, dens_i, right, dens_j, *bufs)
            field[pl.ds(kb, 1), :] += rows
            put(way, t, cols)

        return 0

    lax.fori_loop(0, len(got) * SLOTS, step, 0)


def direct_kernel(near_ref, start, *refs, ways):
    got, (field, *backs), scratch = refs[:ways], refs[ways : 2 * ways + 1], refs[2 * ways + 1 :]

    def clear():
        field[...] = start[...]
        for back in backs:
            back[...] = jnp.zeros_like(back)

    def put(way, t, result):
        for i, back in enumerate(backs):

            @pl.when(way == i)
            def _():
                back[pl.ds(t, 1), :] = result

    near_tiles(clear, near_ref, got, field, put, *scratch)


def far_kernel(pairs, count, row0, row1, own_in, *refs, direct, base):
    got, (rows_out, cols_out), scratch = refs[: len(direct)], refs[len(direct) : -6], refs[-6:]
    rows_out[...] = jnp.zeros_like(rows_out)
    cols_out[...] = jnp.zeros_like(cols_out)
    sources = {0: own_in, **dict(zip(direct, got))}
    far_tiles(pairs, count, (row0, row1), sources, rows_out, cols_out, base, *scratch)


def late_kernel(pairs, count, near_ref, start, row0, row1, rows_in, cols_in, *refs, n_row, direct, late):
    refs = list(refs)
    take = lambda n: [refs.pop(0) for _ in range(n)]
    got, backs = take(len(late)), take(len(direct))
    field, rows_out, cols_out, *messages = take(n_row + 2)
    near_scratch, far_scratch = take(len(NEAR_SCRATCH) + 3), refs
    nfar = cols_out.shape[0]
    base = near_lines(SLOTS, near_ref.shape[1] // 4 - 2)
    my_row = lax.axis_index("row")

    def to_peer(d, lines, value):
        k = lax.rem(jnp.bitwise_xor(my_row, d) - my_row + n_row - 1, n_row)
        for i, message in enumerate(messages):

            @pl.when(k == i)
            def _():
                message[lines, :] = value

    def put(way, t, result):
        for i, d in enumerate(late):
            pl.when(way == i)(lambda: to_peer(d, pl.ds(nfar + t, 1), result))

    def far():
        field[...] = start[...]
        rows_out[...] = rows_in[...]
        cols_out[...] = cols_in[...]
        for message in messages:
            message[nfar:, :] = jnp.zeros((8, BLK), jnp.float32)
        for d, back in zip(direct, backs):
            to_peer(d, slice(nfar, nfar + 8), back[...])
        far_tiles(pairs, count, (row0, row1), dict(zip(late, got)), rows_out, cols_out, base, *far_scratch)
        for message in messages:
            message[0:nfar, :] = cols_out[...]

    near_tiles(far, near_ref, got, field, put, *near_scratch)


def hot(index, blocks, slots, base):
    want = lax.broadcasted_iota(jnp.int32, (blocks, slots), 0) + base * blocks
    return jnp.where(index[:, 0:slots] == want.astype(jnp.float32), 1.0, 0.0)


def spread(pick, slots, weight):
    pick = jnp.concatenate(pick * 3, axis=1).astype(jnp.bfloat16)
    slots = jnp.concatenate(three(jnp.concatenate(slots, axis=0)), axis=0).astype(jnp.bfloat16)
    return jnp.dot(pick, slots, preferred_element_type=jnp.float32) * weight[...]


def cols_kernel(pairs, weight, near, own_far, own_cols, *refs, n_row, base):
    col_far, messages, field = refs[: n_row - 1], refs[n_row - 1 : -1], refs[-1]
    blocks, nfar = weight.shape[0], own_cols.shape[0]
    my_row = lax.axis_index("row")
    line = base + 4 * blocks + 1
    pick = [hot(own_far[blocks, 1:2, :], blocks, nfar, my_row)]
    for k in range(1, n_row):
        way = jnp.bitwise_xor(my_row, lax.rem(my_row + n_row - k, n_row))
        index = jnp.zeros((1, BLK), jnp.float32)
        for d, other in enumerate(col_far):
            index = jnp.where(way == d + 1, other[line : line + 1, :], index)
        pick.append(hot(index, blocks, nfar, my_row))
    field[...] = near[...] + spread(pick, [own_cols[...]] + [m[0:nfar, :] for m in messages], weight)
    for message in messages:
        for t in range(pairs.shape[1] - 1):
            k = lax.rem(pairs[0, t + 1], blocks)
            field[pl.ds(k, 1), :] += message[nfar + t : nfar + t + 1, :]


def rows_kernel(weight, field, row0, row1, *refs, n_col):
    rows, out = refs[:-1], refs[-1]
    blocks, nfar = weight.shape[0], rows[0].shape[0] // 2
    my_col = lax.axis_index("col")
    chips = n_col // 2
    chip = lax.div(my_col, 2)
    pick = []
    for k in range(chips):
        way = jnp.bitwise_xor(chip, lax.rem(chip + chips - k, chips))
        tag = place(way, chips) * (blocks + 1) + blocks
        pick += [hot(half[tag, 0:1, :], blocks, nfar, my_col) for half in (row0, row1)]
    total = field[...] + spread(pick, [r[...] for r in rows], weight)
    for q in range(BLK // LANES):
        out[pl.ds(q, blocks, stride=BLK // LANES), :] = total[:, q * LANES : (q + 1) * LANES]


def f32(*shape):
    return jax.ShapeDtypeStruct(shape, jnp.float32)


def cost(micros):
    return pl.CostEstimate(flops=int(micros * 1.1e9), bytes_accessed=1 << 16, transcendentals=0)


def body(points, density, near_pairs, far_pairs, near_count, far_count, *, n_row, n_col):
    quad = points.shape[1]
    blocks = points.shape[2] // BLK
    nnear, nfar = near_pairs.shape[0], far_pairs.shape[0]
    depth, slots = 4 * quad, nnear - 1
    near_pairs, far_pairs = near_pairs.T, far_pairs.T

    def swap(x, axis, d):
        n = {"row": n_row, "col": n_col}[axis]
        return lax.ppermute(x, axis, [(i, i ^ d) for i in range(n)])

    direct = [d for d in range(1, n_row) if d & (d - 1) == 0]
    late = [d for d in range(1, n_row) if d & (d - 1) != 0]

    def halves(n):
        return [1 << j for j in reversed(range(n.bit_length() - 1))]

    def col_gather(x):
        for d in halves(n_col)[:-1]:
            x = jnp.concatenate([x, swap(x, "col", d)], axis=0)
        return x, swap(x, "col", 1)

    base = near_lines(slots, quad)
    msg_rows = -(-(base + 4 * (blocks + 1)) // 8) * 8
    hbm = (near_pairs, far_pairs, points, density.reshape(-1, LANES))
    hbm = [pltpu.with_memory_space_constraint(x, pltpu.HBM) for x in hbm]
    msg, far_own, near_own, weight = pl.pallas_call(
        prep_kernel,
        out_shape=(
            f32(msg_rows, BLK),
            f32(blocks + 1, 4, BLK),
            f32(blocks, depth + 8, BLK),
            f32(blocks, BLK),
        ),
        in_specs=[HBM, SMEM, HBM, HBM, HBM],
        out_specs=(VMEM, VMEM, VMEM, VMEM),
        scratch_shapes=[
            pltpu.SMEM(near_pairs.shape, jnp.int32),
            pltpu.VMEM(far_pairs.shape, jnp.int32),
            pltpu.VMEM(points.shape, jnp.float32),
            pltpu.VMEM((density.shape[0] // LANES, LANES), jnp.float32),
            pltpu.SemaphoreType.DMA((QUARTERS + 3,)),
        ],
        compiler_params=PARAMS,
        cost_estimate=cost(1.2),
        name="prep",
    )(hbm[0], near_count, *hbm[1:])
    row_far = col_gather(far_own)
    known = {d: swap(msg, "row", d) for d in direct}
    *onward, last = lax.optimization_barrier((*[known[d] for d in direct], row_far[0]))
    known.update(zip(direct, onward))
    row_far = (last, row_far[1])
    for d in late:
        known[d] = swap(known[d ^ (d & -d)], "row", d & -d)
    got = [known[d] for d in range(1, n_row)]

    bufs = [
        pltpu.VMEM((quad * BLK, TERMS), jnp.bfloat16),
        pltpu.VMEM((TERMS, quad * BLK), jnp.bfloat16),
        pltpu.VMEM((BLK, LANES), jnp.float32),
        pltpu.VMEM((8, BLK), jnp.float32),
    ]
    near0 = pl.pallas_call(
        near_own_kernel,
        out_shape=f32(blocks, BLK),
        in_specs=[SMEM, SMEM, VMEM],
        out_specs=VMEM,
        scratch_shapes=bufs,
        compiler_params=PARAMS,
        cost_estimate=cost(5.0),
        name="near_own",
    )(near_pairs, near_count, near_own)

    def near_scratch(n):
        return [
            pltpu.VMEM((depth + 8, BLK), jnp.float32),
            pltpu.SMEM((n, 8, LANES), jnp.float32),
            pltpu.SemaphoreType.DMA((n,)),
        ] + bufs

    far_scratch = [
        pltpu.SMEM((nfar,), jnp.int32),
        pltpu.VMEM((2, 4, BLK), jnp.float32),
        pltpu.VMEM((2, 4, BLK), jnp.float32),
        pltpu.VMEM((2, BLK, TERMS), jnp.bfloat16),
        pltpu.VMEM((2, TERMS, BLK), jnp.bfloat16),
        pltpu.VMEM((2, BLK, LANES), jnp.float32),
    ]
    field, *backs = pl.pallas_call(
        functools.partial(direct_kernel, ways=len(direct)),
        out_shape=[f32(blocks, BLK)] + [f32(8, BLK)] * len(direct),
        in_specs=[VMEM] * (2 + len(direct)),
        out_specs=[VMEM] * (len(direct) + 1),
        scratch_shapes=near_scratch(len(direct)),
        compiler_params=PARAMS,
        cost_estimate=cost(30.0),
        name="near_direct",
    )(near_own, near0, *[got[d - 1] for d in direct])
    far_rows, far_cols = pl.pallas_call(
        functools.partial(far_kernel, direct=direct, base=base),
        out_shape=[f32(nfar, BLK)] * 2,
        in_specs=[SMEM, SMEM] + [VMEM] * (3 + len(direct)),
        out_specs=[VMEM] * 2,
        scratch_shapes=far_scratch,
        compiler_params=PARAMS,
        cost_estimate=cost(3.0),
        name="far_direct",
    )(far_pairs, far_count, *row_far, far_own, *[got[d - 1] for d in direct])
    field, far_rows, far_cols, *messages = pl.pallas_call(
        functools.partial(late_kernel, n_row=n_row, direct=direct, late=late),
        out_shape=[f32(blocks, BLK)] + [f32(nfar, BLK)] * 2 + [f32(nfar + 8, BLK)] * (n_row - 1),
        in_specs=[SMEM, SMEM] + [VMEM] * (6 + n_row - 1),
        out_specs=[VMEM] * (n_row + 2),
        scratch_shapes=near_scratch(len(late)) + far_scratch,
        compiler_params=PARAMS,
        cost_estimate=cost(8.0),
        name="late",
    )(far_pairs, far_count, near_own, field, *row_far, far_rows, far_cols, *[got[d - 1] for d in late], *backs)

    messages = [
        lax.ppermute(x, "row", [(i, (i + k + 1) % n_row) for i in range(n_row)]) for k, x in enumerate(messages)
    ]
    both = jnp.concatenate([far_rows, swap(far_rows, "col", 1)], axis=0)
    rows = [both]
    for k in range(2, n_col, 2):
        rows.append(lax.ppermute(both, "col", [(i, (i + k) % n_col) for i in range(n_col)]))
    field = pl.pallas_call(
        functools.partial(cols_kernel, n_row=n_row, base=base),
        out_shape=f32(blocks, BLK),
        in_specs=[SMEM] + [VMEM] * (2 * n_row + 2),
        out_specs=VMEM,
        compiler_params=PARAMS,
        cost_estimate=cost(1.0),
        name="final_cols",
    )(near_pairs, weight, field, far_own, far_cols, *got, *messages)
    out = pl.pallas_call(
        functools.partial(rows_kernel, n_col=n_col),
        out_shape=f32(blocks * BLK // LANES, LANES),
        in_specs=[VMEM] * (4 + len(rows)),
        out_specs=VMEM,
        compiler_params=PARAMS,
        cost_estimate=cost(1.0),
        name="final_rows",
    )(weight, field, *row_far, *rows)
    return out.reshape(-1)


def solution(mesh):
    in_specs = (
        P(None, None, ("row", "col")),
        P(("row", "col")),
        P(("row", "col"), None),
        P(("row", "col"), None),
        P(("row", "col")),
        P(("row", "col")),
    )
    out_specs = P(("row", "col"))
    kernel = functools.partial(body, n_row=mesh.shape["row"], n_col=mesh.shape["col"])
    return jax.shard_map(kernel, mesh=mesh, in_specs=in_specs, out_specs=out_specs, check_vma=False)
```

profile of v0, /device:TPU:0, one launch (start us, length us, event | category | flops | bytes accessed | tf_op | source)
XLA Modules:
  0.0 50.8 jit_solution(14287180290379231573)
XLA Ops:
  0.7 1.4 %prep.1 = (f32[152,512]{1,0:T(8,128)S(1)}, f32[17,4,512]{2,1,0:T(4,128)S(1)}, f32[16,24,512]{2,1,0:T(8,128)S(1)}, f32[16,512]{1,0:T(8,128)S(1)}) custom-call(s32[2,6]{1,0:T(2,128)} %bitcast.7, s32[1]{0:T(128)S(6)} %copy.10.count, s32[2,16]{1,0:T(2,128)} %bitcast.4, f32[4,4,8192]{2,1,0:T(4,128)} %pts_hbm.1, f32[64,128]{1,0:T(8,128)} %bitcast.10), custom_call_target="tpu_custom_call" | custom-call | flops 1320000000 | bytes 65536 | tf_op jit(solution)/shard_map/prep/pallas_call | solution.py:482
  2.1 3.0 %collective-permute-start.2 = (f32[17,4,512]{2,1,0:T(4,128)S(1)}, f32[17,4,512]{2,1,0:T(4,128)S(1)}, u32[]{:S(2)}, u32[]{:S(2)}) collective-permute-start(f32[17,4,512]{2,1,0:T(4,128)S(1)} %get-tuple-element.26.own_in.own_far), channel_id=1, source_target_pairs={{0,4},{1,5},{2,6},{3,7},{4,0},{5,1},{6,2},{7,3},{8,12},{9,13},{10,... | collective-permute-start | bytes 417800 | tf_op jit(solution)/shard_map/ppermute | solution.py:465
  5.1 2.6 %collective-permute-start.1 = (f32[152,512]{1,0:T(8,128)S(1)}, f32[152,512]{1,0:T(8,128)S(1)}, u32[]{:S(2)}, u32[]{:S(2)}) collective-permute-start(f32[152,512]{1,0:T(8,128)S(1)} %get-tuple-element.25), channel_id=1, source_target_pairs={{0,16},{8,24},{16,0},{24,8},{1,17},{9,25},{17,1},{25,9},{2,18},{10... | collective-permute-start | bytes 933896 | tf_op jit(solution)/shard_map/ppermute | solution.py:465
  7.7 1.6 %collective-permute-start = (f32[152,512]{1,0:T(8,128)S(1)}, f32[152,512]{1,0:T(8,128)S(1)}, u32[]{:S(2)}, u32[]{:S(2)}) collective-permute-start(f32[152,512]{1,0:T(8,128)S(1)} %get-tuple-element.25), channel_id=1, source_target_pairs={{0,8},{8,0},{16,24},{24,16},{1,9},{9,1},{17,25},{25,17},{2,10},{10... | collective-permute-start | bytes 933896 | tf_op jit(solution)/shard_map/ppermute | solution.py:465
  9.3 0.0 collective-permute-done.2
  9.3 0.1 pad_maximum_fusion
  9.4 0.0 copy-start.1
  9.4 1.6 %collective-permute-start.3 = (f32[34,4,512]{2,1,0:T(4,128)S(1)}, f32[34,4,512]{2,1,0:T(4,128)S(1)}, u32[]{:S(2)}, u32[]{:S(2)}) collective-permute-start(f32[34,4,512]{2,1,0:T(4,128)S(1)} %pad_maximum_fusion), channel_id=1, source_target_pairs={{0,2},{1,3},{2,0},{3,1},{4,6},{5,7},{6,4},{7,5},{8,10},{9,11},{10,... | collective-permute-start | bytes 835592 | tf_op jit(solution)/shard_map/ppermute | solution.py:465
  10.9 0.0 copy-done.1
  10.9 3.5 %near_own.1.start = f32[16,512]{1,0:T(8,128)S(1)} custom-call(s32[2,6]{1,0:T(2,128)S(1)} %bitcast.8, s32[1]{0:T(128)S(6)} %copy.10.count, f32[16,24,512]{2,1,0:T(8,128)S(1)} %get-tuple-element.24.near_ref), custom_call_target="tpu_custom_call" | custom-call | flops 5500000256 | bytes 65536 | tf_op jit(solution)/shard_map/near_own/pallas_call | solution.py:518
  15.1 1.9 %collective-permute-done.3 = f32[34,4,512]{2,1,0:T(4,128)S(1)} collective-permute-done((f32[34,4,512]{2,1,0:T(4,128)S(1)}, f32[34,4,512]{2,1,0:T(4,128)S(1)}, u32[]{:S(2)}, u32[]{:S(2)}) %collective-permute-start.3) | collective-permute-done | bytes 278560 | tf_op jit(solution)/shard_map/ppermute | solution.py:465
  17.0 0.0 copy-start
  17.0 0.1 collective-permute-start.4
  17.1 4.5 %collective-permute-done.1.refs_1_ = f32[152,512]{1,0:T(8,128)S(1)} collective-permute-done((f32[152,512]{1,0:T(8,128)S(1)}, f32[152,512]{1,0:T(8,128)S(1)}, u32[]{:S(2)}, u32[]{:S(2)}) %collective-permute-start.1) | collective-permute-done | bytes 311328 | tf_op jit(solution)/shard_map/ppermute | solution.py:465
  21.6 0.2 collective-permute-done.refs_0_
  21.8 1.4 %collective-permute-start.5 = (f32[152,512]{1,0:T(8,128)S(1)}, f32[152,512]{1,0:T(8,128)S(1)}, u32[]{:S(2)}, u32[]{:S(2)}) collective-permute-start(f32[152,512]{1,0:T(8,128)S(1)} %collective-permute-done.1.refs_1_), channel_id=1, source_target_pairs={{0,8},{8,0},{16,24},{24,16},{1,9},{9,1},{17,25},{25,17},{2,10},{10... | collective-permute-start | bytes 933896 | tf_op jit(solution)/shard_map/ppermute | solution.py:465
  23.2 0.9 %near_direct.1 = (f32[16,512]{1,0:T(8,128)S(1)}, f32[8,512]{1,0:T(8,128)S(1)}, f32[8,512]{1,0:T(8,128)S(1)}) custom-call(f32[16,24,512]{2,1,0:T(8,128)S(1)} %get-tuple-element.24.near_ref, f32[16,512]{1,0:T(8,128)S(1)} %near_own.1.start, f32[152,512]{1,0:T(8,128)S(1)} %collective-permute-done.refs_0_, f32[152,512]{1,0:T(8,128)S(1)} %collective-permute-done.1.refs_1_), custom_call_target="tpu_custom_call" | custom-call | flops 32999999488 | bytes 65536 | tf_op jit(solution)/shard_map/near_direct/pallas_call | solution.py:544
  24.2 0.0 collective-permute-done.4.row1
  24.2 0.0 copy-done
  24.2 4.5 %far_direct.1 = (f32[16,512]{1,0:T(8,128)S(1)}, f32[16,512]{1,0:T(8,128)S(1)}) custom-call(s32[2,16]{1,0:T(2,128)S(1)} %bitcast.5, s32[1]{0:T(128)S(6)} %copy.11.count, f32[68,4,512]{2,1,0:T(4,128)S(1)} %constant_dynamic-update-slice_fusion.row0, f32[68,4,512]{2,1,0:T(4,128)S(1)} %collective-permute-done.4.row1, ...), custom_call_target="tpu_custom_call" | custom-call | flops 3300000000 | bytes 65536 | tf_op jit(solution)/shard_map/far_direct/pallas_call | solution.py:554
  28.8 1.0 %collective-permute-done.5.refs_0_.refs_2_ = f32[152,512]{1,0:T(8,128)S(1)} collective-permute-done((f32[152,512]{1,0:T(8,128)S(1)}, f32[152,512]{1,0:T(8,128)S(1)}, u32[]{:S(2)}, u32[]{:S(2)}) %collective-permute-start.5) | collective-permute-done | bytes 311328 | tf_op jit(solution)/shard_map/ppermute | solution.py:465
  29.8 4.2 %late.1 = (f32[16,512]{1,0:T(8,128)S(1)}, f32[16,512]{1,0:T(8,128)S(1)}, f32[16,512]{1,0:T(8,128)S(1)}, f32[24,512]{1,0:T(8,128)S(1)}, f32[24,512]{1,0:T(8,128)S(1)}, /*index=5*/f32[24,512]{1,0:T(8,128)S(1)}) custom-call(s32[2,16]{1,0:T(2,128)S(1)} %bitcast.6, s32[1]{0:T(128)S(6)} %copy.11.count, f32[16,24,512]{2,1,0:T(8,128)S(1)} %get-tuple-element.24.near_ref, ...), custom_call_target="tpu_custom_call" | custom-call | flops 8800000000 | bytes 65536 | tf_op jit(solution)/shard_map/late/pallas_call | solution.py:564
  34.0 0.1 collective-permute-start.9
  34.1 2.1 %collective-permute-start.6 = (f32[24,512]{1,0:T(8,128)S(1)}, f32[24,512]{1,0:T(8,128)S(1)}, u32[]{:S(2)}, u32[]{:S(2)}) collective-permute-start(f32[24,512]{1,0:T(8,128)S(1)} %get-tuple-element.37), channel_id=1, source_target_pairs={{0,8},{8,16},{16,24},{24,0},{1,9},{9,17},{17,25},{25,1},{2,10},{10... | collective-permute-start | bytes 147464 | tf_op jit(solution)/shard_map/ppermute | solution.py:576
  36.2 1.7 %collective-permute-start.7 = (f32[24,512]{1,0:T(8,128)S(1)}, f32[24,512]{1,0:T(8,128)S(1)}, u32[]{:S(2)}, u32[]{:S(2)}) collective-permute-start(f32[24,512]{1,0:T(8,128)S(1)} %get-tuple-element.38), channel_id=1, source_target_pairs={{0,16},{8,24},{16,0},{24,8},{1,17},{9,25},{17,1},{25,9},{2,18},{10... | collective-permute-start | bytes 147464 | tf_op jit(solution)/shard_map/ppermute | solution.py:576
  37.9 0.7 %collective-permute-start.8 = (f32[24,512]{1,0:T(8,128)S(1)}, f32[24,512]{1,0:T(8,128)S(1)}, u32[]{:S(2)}, u32[]{:S(2)}) collective-permute-start(f32[24,512]{1,0:T(8,128)S(1)} %get-tuple-element.39), channel_id=1, source_target_pairs={{0,24},{8,0},{16,8},{24,16},{1,25},{9,1},{17,9},{25,17},{2,26},{10... | collective-permute-start | bytes 147464 | tf_op jit(solution)/shard_map/ppermute | solution.py:576
  38.6 0.0 collective-permute-done.9
  38.6 6.1 %collective-permute-start.12 = (f32[32,512]{1,0:T(8,128)S(1)}, f32[32,512]{1,0:T(8,128)S(1)}, u32[]{:S(2)}, u32[]{:S(2)}) collective-permute-start(f32[32,512]{1,0:T(8,128)S(1)} %constant_dynamic-update-slice_fusion.3.refs_0_), channel_id=1, source_target_pairs={{0,6},{1,7},{2,0},{3,1},{4,2},{5,3},{6,4},{7,5},{8,14},{9,15},{10,... | collective-permute-start | bytes 196616 | tf_op jit(solution)/shard_map/ppermute | solution.py:581
  44.8 0.0 collective-permute-start.11
  44.8 0.0 collective-permute-done.6.refs_3_
  44.8 0.6 %collective-permute-start.10 = (f32[32,512]{1,0:T(8,128)S(1)}, f32[32,512]{1,0:T(8,128)S(1)}, u32[]{:S(2)}, u32[]{:S(2)}) collective-permute-start(f32[32,512]{1,0:T(8,128)S(1)} %constant_dynamic-update-slice_fusion.3.refs_0_), channel_id=1, source_target_pairs={{0,2},{1,3},{2,4},{3,5},{4,6},{5,7},{6,0},{7,1},{8,10},{9,11},{10,... | collective-permute-start | bytes 196616 | tf_op jit(solution)/shard_map/ppermute | solution.py:581
  45.4 0.0 collective-permute-done.7.refs_4_
  45.4 0.0 collective-permute-done.8.refs_5_
  45.4 0.8 %final_cols.1.field = f32[16,512]{1,0:T(8,128)S(1)} custom-call(s32[2,6]{1,0:T(2,128)S(1)} %bitcast.9, f32[16,512]{1,0:T(8,128)S(1)} %get-tuple-element.23.weight, f32[16,512]{1,0:T(8,128)S(1)} %get-tuple-element.35.near, f32[17,4,512]{2,1,0:T(4,128)S(1)} %get-tuple-element.26.own_in.own_far, f32[16,512]{1,0:T(8,128)S(1)} %get-tuple-element.36.own_cols, ...), custom_call_target="tpu_custom_call" | custom-call | flops 1100000000 | bytes 65536 | tf_op jit(solution)/shard_map/final_cols/pallas_call | solution.py:582
  46.2 0.5 collective-permute-done.12.refs_3_
  46.7 2.4 %collective-permute-done.11.refs_2_ = f32[32,512]{1,0:T(8,128)S(1)} collective-permute-done((f32[32,512]{1,0:T(8,128)S(1)}, f32[32,512]{1,0:T(8,128)S(1)}, u32[]{:S(2)}, u32[]{:S(2)}) %collective-permute-start.11) | collective-permute-done | bytes 65568 | tf_op jit(solution)/shard_map/ppermute | solution.py:581
  49.0 0.9 %collective-permute-done.10.refs_1_ = f32[32,512]{1,0:T(8,128)S(1)} collective-permute-done((f32[32,512]{1,0:T(8,128)S(1)}, f32[32,512]{1,0:T(8,128)S(1)}, u32[]{:S(2)}, u32[]{:S(2)}) %collective-permute-start.10) | collective-permute-done | bytes 65568 | tf_op jit(solution)/shard_map/ppermute | solution.py:581
  49.9 0.9 %final_rows.1 = f32[64,128]{1,0:T(8,128)} custom-call(f32[16,512]{1,0:T(8,128)S(1)} %get-tuple-element.23.weight, f32[16,512]{1,0:T(8,128)S(1)} %final_cols.1.field, f32[68,4,512]{2,1,0:T(4,128)S(1)} %constant_dynamic-update-slice_fusion.row0, f32[68,4,512]{2,1,0:T(4,128)S(1)} %collective-permute-done.4.row1, ...), custom_call_target="tpu_custom_call" | custom-call | flops 1100000000 | bytes 65536 | tf_op jit(solution)/shard_map/final_rows/pallas_call | solution.py:591
  (5 shorter events, 0.1 us)
Async XLA Ops:
  2.1 7.2 %collective-permute-start.2 = (f32[17,4,512]{2,1,0:T(4,128)S(1)}, f32[17,4,512]{2,1,0:T(4,128)S(1)}, u32[]{:S(2)}, u32[]{:S(2)}) collective-permute-start(f32[17,4,512]{2,1,0:T(4,128)S(1)} %get-tuple-element.26.own_in.own_far), channel_id=1, source_target_pairs={{0,4},{1,5},{2,6},{3,7},{4,0},{5,1},{6,2},{7,3},{8,12},{9,13},{10,... | collective-permute-start | bytes 417800 | tf_op jit(solution)/shard_map/ppermute | solution.py:465
  5.1 16.5 %collective-permute-start.1 = (f32[152,512]{1,0:T(8,128)S(1)}, f32[152,512]{1,0:T(8,128)S(1)}, u32[]{:S(2)}, u32[]{:S(2)}) collective-permute-start(f32[152,512]{1,0:T(8,128)S(1)} %get-tuple-element.25), channel_id=1, source_target_pairs={{0,16},{8,24},{16,0},{24,8},{1,17},{9,25},{17,1},{25,9},{2,18},{10... | collective-permute-start | bytes 933896 | tf_op jit(solution)/shard_map/ppermute | solution.py:465
  7.7 14.1 %collective-permute-start = (f32[152,512]{1,0:T(8,128)S(1)}, f32[152,512]{1,0:T(8,128)S(1)}, u32[]{:S(2)}, u32[]{:S(2)}) collective-permute-start(f32[152,512]{1,0:T(8,128)S(1)} %get-tuple-element.25), channel_id=1, source_target_pairs={{0,8},{8,0},{16,24},{24,16},{1,9},{9,1},{17,25},{25,17},{2,10},{10... | collective-permute-start | bytes 933896 | tf_op jit(solution)/shard_map/ppermute | solution.py:465
  9.4 1.6 %copy-start.1 = (s32[6,2]{0,1:T(2,128)S(1)}, s32[6,2]{0,1:T(2,128)}, u32[]{:S(2)}) copy-start(s32[6,2]{0,1:T(2,128)} %param.8) | copy-start | bytes 148
  9.4 7.6 %collective-permute-start.3 = (f32[34,4,512]{2,1,0:T(4,128)S(1)}, f32[34,4,512]{2,1,0:T(4,128)S(1)}, u32[]{:S(2)}, u32[]{:S(2)}) collective-permute-start(f32[34,4,512]{2,1,0:T(4,128)S(1)} %pad_maximum_fusion), channel_id=1, source_target_pairs={{0,2},{1,3},{2,0},{3,1},{4,6},{5,7},{6,4},{7,5},{8,10},{9,11},{10,... | collective-permute-start | bytes 835592 | tf_op jit(solution)/shard_map/ppermute | solution.py:465
  17.0 7.2 %copy-start = (s32[16,2]{0,1:T(2,128)S(1)}, s32[16,2]{0,1:T(2,128)}, u32[]{:S(2)}) copy-start(s32[16,2]{0,1:T(2,128)} %param.9) | copy-start | bytes 388
  17.0 7.2 %collective-permute-start.4 = (f32[68,4,512]{2,1,0:T(4,128)S(1)}, f32[68,4,512]{2,1,0:T(4,128)S(1)}, u32[]{:S(2)}, u32[]{:S(2)}) collective-permute-start(f32[68,4,512]{2,1,0:T(4,128)S(1)} %constant_dynamic-update-slice_fusion.row0), channel_id=1, source_target_pairs={{0,1},{1,0},{2,3},{3,2},{4,5},{5,4},{6,7},{7,6},{8,9},{9,8},{10,11... | collective-permute-start | bytes 1671176 | tf_op jit(solution)/shard_map/ppermute | solution.py:465
  21.8 8.0 %collective-permute-start.5 = (f32[152,512]{1,0:T(8,128)S(1)}, f32[152,512]{1,0:T(8,128)S(1)}, u32[]{:S(2)}, u32[]{:S(2)}) collective-permute-start(f32[152,512]{1,0:T(8,128)S(1)} %collective-permute-done.1.refs_1_), channel_id=1, source_target_pairs={{0,8},{8,0},{16,24},{24,16},{1,9},{9,1},{17,25},{25,17},{2,10},{10... | collective-permute-start | bytes 933896 | tf_op jit(solution)/shard_map/ppermute | solution.py:465
  34.0 4.6 %collective-permute-start.9 = (f32[16,512]{1,0:T(8,128)S(1)}, f32[16,512]{1,0:T(8,128)S(1)}, u32[]{:S(2)}, u32[]{:S(2)}) collective-permute-start(f32[16,512]{1,0:T(8,128)S(1)} %get-tuple-element.40), channel_id=1, source_target_pairs={{0,1},{1,0},{2,3},{3,2},{4,5},{5,4},{6,7},{7,6},{8,9},{9,8},{10,11... | collective-permute-start | bytes 98312 | tf_op jit(solution)/shard_map/ppermute | solution.py:465
  34.1 10.7 %collective-permute-start.6 = (f32[24,512]{1,0:T(8,128)S(1)}, f32[24,512]{1,0:T(8,128)S(1)}, u32[]{:S(2)}, u32[]{:S(2)}) collective-permute-start(f32[24,512]{1,0:T(8,128)S(1)} %get-tuple-element.37), channel_id=1, source_target_pairs={{0,8},{8,16},{16,24},{24,0},{1,9},{9,17},{17,25},{25,1},{2,10},{10... | collective-permute-start | bytes 147464 | tf_op jit(solution)/shard_map/ppermute | solution.py:576
  36.2 9.2 %collective-permute-start.7 = (f32[24,512]{1,0:T(8,128)S(1)}, f32[24,512]{1,0:T(8,128)S(1)}, u32[]{:S(2)}, u32[]{:S(2)}) collective-permute-start(f32[24,512]{1,0:T(8,128)S(1)} %get-tuple-element.38), channel_id=1, source_target_pairs={{0,16},{8,24},{16,0},{24,8},{1,17},{9,25},{17,1},{25,9},{2,18},{10... | collective-permute-start | bytes 147464 | tf_op jit(solution)/shard_map/ppermute | solution.py:576
  37.9 7.5 %collective-permute-start.8 = (f32[24,512]{1,0:T(8,128)S(1)}, f32[24,512]{1,0:T(8,128)S(1)}, u32[]{:S(2)}, u32[]{:S(2)}) collective-permute-start(f32[24,512]{1,0:T(8,128)S(1)} %get-tuple-element.39), channel_id=1, source_target_pairs={{0,24},{8,0},{16,8},{24,16},{1,25},{9,1},{17,9},{25,17},{2,26},{10... | collective-permute-start | bytes 147464 | tf_op jit(solution)/shard_map/ppermute | solution.py:576
  38.6 8.0 %collective-permute-start.12 = (f32[32,512]{1,0:T(8,128)S(1)}, f32[32,512]{1,0:T(8,128)S(1)}, u32[]{:S(2)}, u32[]{:S(2)}) collective-permute-start(f32[32,512]{1,0:T(8,128)S(1)} %constant_dynamic-update-slice_fusion.3.refs_0_), channel_id=1, source_target_pairs={{0,6},{1,7},{2,0},{3,1},{4,2},{5,3},{6,4},{7,5},{8,14},{9,15},{10,... | collective-permute-start | bytes 196616 | tf_op jit(solution)/shard_map/ppermute | solution.py:581
  44.8 4.3 %collective-permute-start.11 = (f32[32,512]{1,0:T(8,128)S(1)}, f32[32,512]{1,0:T(8,128)S(1)}, u32[]{:S(2)}, u32[]{:S(2)}) collective-permute-start(f32[32,512]{1,0:T(8,128)S(1)} %constant_dynamic-update-slice_fusion.3.refs_0_), channel_id=1, source_target_pairs={{0,4},{1,5},{2,6},{3,7},{4,0},{5,1},{6,2},{7,3},{8,12},{9,13},{10,... | collective-permute-start | bytes 196616 | tf_op jit(solution)/shard_map/ppermute | solution.py:581
  44.8 5.2 %collective-permute-start.10 = (f32[32,512]{1,0:T(8,128)S(1)}, f32[32,512]{1,0:T(8,128)S(1)}, u32[]{:S(2)}, u32[]{:S(2)}) collective-permute-start(f32[32,512]{1,0:T(8,128)S(1)} %constant_dynamic-update-slice_fusion.3.refs_0_), channel_id=1, source_target_pairs={{0,2},{1,3},{2,4},{3,5},{4,6},{5,7},{6,0},{7,1},{8,10},{9,11},{10,... | collective-permute-start | bytes 196616 | tf_op jit(solution)/shard_map/ppermute | solution.py:581
where the time goes:
time: 51 us; the launch traced here: 50.8 us
  starting transfers between devices  21.6 us (42%)
  Pallas kernels  16.3 us (32%)
  waiting for transfers between devices  11.3 us (22%)
  between operations  1.43 us (3%)
    ppermute x7, starting transfers between devices, swap(): return lax.ppermute(x, axis, [(i, i ^ d) for i in range(n)])  10.3 us
    ppermute x7, waiting for transfers between devices, swap(): return lax.ppermute(x, axis, [(i, i ^ d) for i in range(n)])  7.55 us
    ppermute x3, starting transfers between devices, body(): lax.ppermute(both, 'col', [(i, (i + k) % n_col) for i in range(n_col)])  6.77 us
    pallas_call x1, Pallas kernels, body(): pl.pallas_call(functools.partial(far_kernel, direct=direct, base=base), o...  4.55 us
    ppermute x3, starting transfers between devices, body(): lax.ppermute(x, 'row', [(i, (i + k + 1) % n_row) for i in range(n_row)])  4.54 us
    pallas_call x1, Pallas kernels, body(): pl.pallas_call(functools.partial(late_kernel, n_row=n_row, direct=direct,...  4.22 us
    ppermute x3, waiting for transfers between devices, body(): lax.ppermute(both, 'col', [(i, (i + k) % n_col) for i in range(n_col)])  3.72 us
    pallas_call x1, Pallas kernels, body(): pl.pallas_call(near_own_kernel, out_shape=f32(blocks, BLK), in_specs=[SME...  3.49 us
  transfers between devices with their start and end apart: 13, of which 7 were waited for; matrix products, arithmetic and copies ran while one was open for 0% of the time, Pallas kernels for 19%

commit v1 on v0

--- a/solution.py
+++ b/solution.py
@@ -437,7 +437,7 @@
     chip = lax.div(my_col, 2)
     pick = []
     for k in range(chips):
-        way = jnp.bitwise_xor(chip, lax.rem(chip + chips - k, chips))
+        way = jnp.bitwise_xor(chip, lax.rem(chip + k, chips))
         tag = place(way, chips) * (blocks + 1) + blocks
         pick += [hot(half[tag, 0:1, :], blocks, nfar, my_col) for half in (row0, row1)]
     total = field[...] + spread(pick, [r[...] for r in rows], weight)
@@ -502,9 +502,10 @@
     )(hbm[0], near_count, *hbm[1:])
     row_far = col_gather(far_own)
     known = {d: swap(msg, "row", d) for d in direct}
-    *onward, last = lax.optimization_barrier((*[known[d] for d in direct], row_far[0]))
-    known.update(zip(direct, onward))
-    row_far = (last, row_far[1])
+    passed = [d for d in direct if d > 1]
+    *onward, first = lax.optimization_barrier((*[known[d] for d in passed], row_far[0]))
+    known.update(zip(passed, onward))
+    row_far = (first, row_far[1])
     for d in late:
         known[d] = swap(known[d ^ (d & -d)], "row", d & -d)
     got = [known[d] for d in range(1, n_row)]
@@ -578,7 +579,7 @@
     both = jnp.concatenate([far_rows, swap(far_rows, "col", 1)], axis=0)
     rows = [both]
     for k in range(2, n_col, 2):
-        rows.append(lax.ppermute(both, "col", [(i, (i + k) % n_col) for i in range(n_col)]))
+        rows.append(lax.ppermute(both, "col", [(i, (i - k) % n_col) for i in range(n_col)]))
     field = pl.pallas_call(
         functools.partial(cols_kernel, n_row=n_row, base=base),
         out_shape=f32(blocks, BLK),

time: 51 us -> 50.8 us (level)
    ppermute x3, waiting for transfers between devices: 3.72 us -> 1.07 us  [body(): lax.ppermute(both, 'col', [(i, (i - k) % n_col) for i in range(n_col)])]
    ppermute x7, waiting for transfers between devices: 7.55 us -> 9.72 us  [swap(): return lax.ppermute(x, axis, [(i, i ^ d) for i in range(n)])]
    pallas_call x1, Pallas kernels: 4.22 us -> 5.9 us  [body(): pl.pallas_call(functools.partial(late_kernel, n_row=n_row, direct=direct,...]
    ppermute x3, starting transfers between devices: 6.77 us -> 8.29 us  [body(): lax.ppermute(both, 'col', [(i, (i - k) % n_col) for i in range(n_col)])]
    pallas_call x1, Pallas kernels: 4.55 us -> 3.27 us  [body(): pl.pallas_call(functools.partial(far_kernel, direct=direct, base=base), o...]
    ppermute x7, starting transfers between devices: 10.3 us -> 9.46 us  [swap(): return lax.ppermute(x, axis, [(i, i ^ d) for i in range(n)])]
    ppermute x3, starting transfers between devices: 4.54 us -> 3.88 us  [body(): lax.ppermute(x, 'row', [(i, (i + k + 1) % n_row) for i in range(n_row)])]
  transfers between devices with their start and end apart: 13 -> 13, of which waited for: 7 -> 4; matrix products, arithmetic and copies ran while one was open for 0% -> 0% of each run, Pallas kernels for 19% -> 17%
where the time goes in v1:
time: 50.8 us; the launch traced here: 50.7 us
  starting transfers between devices  21.6 us (43%)
  Pallas kernels  16.7 us (33%)
  waiting for transfers between devices  10.8 us (21%)
  between operations  1.44 us (3%)
    ppermute x7, waiting for transfers between devices, swap(): return lax.ppermute(x, axis, [(i, i ^ d) for i in range(n)])  9.72 us
    ppermute x7, starting transfers between devices, swap(): return lax.ppermute(x, axis, [(i, i ^ d) for i in range(n)])  9.46 us
    ppermute x3, starting transfers between devices, body(): lax.ppermute(both, 'col', [(i, (i - k) % n_col) for i in range(n_col)])  8.29 us
    pallas_call x1, Pallas kernels, body(): pl.pallas_call(functools.partial(late_kernel, n_row=n_row, direct=direct,...  5.9 us
    ppermute x3, starting transfers between devices, body(): lax.ppermute(x, 'row', [(i, (i + k + 1) % n_row) for i in range(n_row)])  3.88 us
    pallas_call x1, Pallas kernels, body(): pl.pallas_call(near_own_kernel, out_shape=f32(blocks, BLK), in_specs=[SME...  3.46 us
    pallas_call x1, Pallas kernels, body(): pl.pallas_call(functools.partial(far_kernel, direct=direct, base=base), o...  3.27 us
    pallas_call x1, Pallas kernels, body(): pl.pallas_call(prep_kernel, out_shape=(f32(msg_rows, BLK), f32(blocks + 1...  1.43 us
  transfers between devices with their start and end apart: 13, of which 4 were waited for; matrix products, arithmetic and copies ran while one was open for 0% of the time, Pallas kernels for 17%

profile of v1, /device:TPU:0, one launch (start us, length us, event | category | flops | bytes accessed | tf_op | source)
XLA Modules:
  0.0 50.7 jit_solution(8011546317352232560)
XLA Ops:
  0.7 1.4 %prep.1 = (f32[152,512]{1,0:T(8,128)S(1)}, f32[17,4,512]{2,1,0:T(4,128)S(1)}, f32[16,24,512]{2,1,0:T(8,128)S(1)}, f32[16,512]{1,0:T(8,128)S(1)}) custom-call(s32[2,6]{1,0:T(2,128)} %bitcast.7, s32[1]{0:T(128)S(6)} %copy.10.count, s32[2,16]{1,0:T(2,128)} %bitcast.4, f32[4,4,8192]{2,1,0:T(4,128)} %pts_hbm.1, f32[64,128]{1,0:T(8,128)} %bitcast.10), custom_call_target="tpu_custom_call" | custom-call | flops 1320000000 | bytes 65536 | tf_op jit(solution)/shard_map/prep/pallas_call | solution.py:482
  2.1 3.0 %collective-permute-start.2 = (f32[17,4,512]{2,1,0:T(4,128)S(1)}, f32[17,4,512]{2,1,0:T(4,128)S(1)}, u32[]{:S(2)}, u32[]{:S(2)}) collective-permute-start(f32[17,4,512]{2,1,0:T(4,128)S(1)} %get-tuple-element.25.own_in.own_far), channel_id=1, source_target_pairs={{0,4},{1,5},{2,6},{3,7},{4,0},{5,1},{6,2},{7,3},{8,12},{9,13},{10,... | collective-permute-start | bytes 417800 | tf_op jit(solution)/shard_map/ppermute | solution.py:465
  5.1 2.6 %collective-permute-start.1 = (f32[152,512]{1,0:T(8,128)S(1)}, f32[152,512]{1,0:T(8,128)S(1)}, u32[]{:S(2)}, u32[]{:S(2)}) collective-permute-start(f32[152,512]{1,0:T(8,128)S(1)} %get-tuple-element.24), channel_id=1, source_target_pairs={{0,16},{8,24},{16,0},{24,8},{1,17},{9,25},{17,1},{25,9},{2,18},{10... | collective-permute-start | bytes 933896 | tf_op jit(solution)/shard_map/ppermute | solution.py:465
  7.7 1.6 %collective-permute-start = (f32[152,512]{1,0:T(8,128)S(1)}, f32[152,512]{1,0:T(8,128)S(1)}, u32[]{:S(2)}, u32[]{:S(2)}) collective-permute-start(f32[152,512]{1,0:T(8,128)S(1)} %get-tuple-element.24), channel_id=1, source_target_pairs={{0,8},{8,0},{16,24},{24,16},{1,9},{9,1},{17,25},{25,17},{2,10},{10... | collective-permute-start | bytes 933896 | tf_op jit(solution)/shard_map/ppermute | solution.py:465
  9.3 0.0 collective-permute-done.2
  9.3 0.1 pad_maximum_fusion
  9.4 0.0 copy-start.1
  9.4 1.6 %collective-permute-start.3 = (f32[34,4,512]{2,1,0:T(4,128)S(1)}, f32[34,4,512]{2,1,0:T(4,128)S(1)}, u32[]{:S(2)}, u32[]{:S(2)}) collective-permute-start(f32[34,4,512]{2,1,0:T(4,128)S(1)} %pad_maximum_fusion), channel_id=1, source_target_pairs={{0,2},{1,3},{2,0},{3,1},{4,6},{5,7},{6,4},{7,5},{8,10},{9,11},{10,... | collective-permute-start | bytes 835592 | tf_op jit(solution)/shard_map/ppermute | solution.py:465
  10.9 0.0 copy-done.1
  10.9 3.5 %near_own.1.start = f32[16,512]{1,0:T(8,128)S(1)} custom-call(s32[2,6]{1,0:T(2,128)S(1)} %bitcast.8, s32[1]{0:T(128)S(6)} %copy.10.count, f32[16,24,512]{2,1,0:T(8,128)S(1)} %get-tuple-element.23.near_ref), custom_call_target="tpu_custom_call" | custom-call | flops 5500000256 | bytes 65536 | tf_op jit(solution)/shard_map/near_own/pallas_call | solution.py:519
  15.1 1.9 %collective-permute-done.3 = f32[34,4,512]{2,1,0:T(4,128)S(1)} collective-permute-done((f32[34,4,512]{2,1,0:T(4,128)S(1)}, f32[34,4,512]{2,1,0:T(4,128)S(1)}, u32[]{:S(2)}, u32[]{:S(2)}) %collective-permute-start.3) | collective-permute-done | bytes 278560 | tf_op jit(solution)/shard_map/ppermute | solution.py:465
  17.0 0.0 copy-start
  17.0 0.1 collective-permute-start.4
  17.1 4.5 %collective-permute-done.1.refs_1_ = f32[152,512]{1,0:T(8,128)S(1)} collective-permute-done((f32[152,512]{1,0:T(8,128)S(1)}, f32[152,512]{1,0:T(8,128)S(1)}, u32[]{:S(2)}, u32[]{:S(2)}) %collective-permute-start.1) | collective-permute-done | bytes 311328 | tf_op jit(solution)/shard_map/ppermute | solution.py:465
  21.6 0.6 %collective-permute-start.5 = (f32[152,512]{1,0:T(8,128)S(1)}, f32[152,512]{1,0:T(8,128)S(1)}, u32[]{:S(2)}, u32[]{:S(2)}) collective-permute-start(f32[152,512]{1,0:T(8,128)S(1)} %collective-permute-done.1.refs_1_), channel_id=1, source_target_pairs={{0,8},{8,0},{16,24},{24,16},{1,9},{9,1},{17,25},{25,17},{2,10},{10... | collective-permute-start | bytes 933896 | tf_op jit(solution)/shard_map/ppermute | solution.py:465
  22.2 0.0 collective-permute-done.refs_0_
  22.2 0.9 %near_direct.1 = (f32[16,512]{1,0:T(8,128)S(1)}, f32[8,512]{1,0:T(8,128)S(1)}, f32[8,512]{1,0:T(8,128)S(1)}) custom-call(f32[16,24,512]{2,1,0:T(8,128)S(1)} %get-tuple-element.23.near_ref, f32[16,512]{1,0:T(8,128)S(1)} %near_own.1.start, f32[152,512]{1,0:T(8,128)S(1)} %collective-permute-done.refs_0_, f32[152,512]{1,0:T(8,128)S(1)} %collective-permute-done.1.refs_1_), custom_call_target="tpu_custom_call" | custom-call | flops 32999999488 | bytes 65536 | tf_op jit(solution)/shard_map/near_direct/pallas_call | solution.py:545
  23.1 0.0 collective-permute-done.4.row1
  23.2 0.0 copy-done
  23.2 3.3 %far_direct.1 = (f32[16,512]{1,0:T(8,128)S(1)}, f32[16,512]{1,0:T(8,128)S(1)}) custom-call(s32[2,16]{1,0:T(2,128)S(1)} %bitcast.5, s32[1]{0:T(128)S(6)} %copy.11.count, f32[68,4,512]{2,1,0:T(4,128)S(1)} %constant_dynamic-update-slice_fusion.row0, f32[68,4,512]{2,1,0:T(4,128)S(1)} %collective-permute-done.4.row1, ...), custom_call_target="tpu_custom_call" | custom-call | flops 3300000000 | bytes 65536 | tf_op jit(solution)/shard_map/far_direct/pallas_call | solution.py:555
  26.4 3.3 %collective-permute-done.5.refs_0_.refs_2_ = f32[152,512]{1,0:T(8,128)S(1)} collective-permute-done((f32[152,512]{1,0:T(8,128)S(1)}, f32[152,512]{1,0:T(8,128)S(1)}, u32[]{:S(2)}, u32[]{:S(2)}) %collective-permute-start.5) | collective-permute-done | bytes 311328 | tf_op jit(solution)/shard_map/ppermute | solution.py:465
  29.8 5.9 %late.1 = (f32[16,512]{1,0:T(8,128)S(1)}, f32[16,512]{1,0:T(8,128)S(1)}, f32[16,512]{1,0:T(8,128)S(1)}, f32[24,512]{1,0:T(8,128)S(1)}, f32[24,512]{1,0:T(8,128)S(1)}, /*index=5*/f32[24,512]{1,0:T(8,128)S(1)}) custom-call(s32[2,16]{1,0:T(2,128)S(1)} %bitcast.6, s32[1]{0:T(128)S(6)} %copy.11.count, f32[16,24,512]{2,1,0:T(8,128)S(1)} %get-tuple-element.23.near_ref, ...), custom_call_target="tpu_custom_call" | custom-call | flops 8800000000 | bytes 65536 | tf_op jit(solution)/shard_map/late/pallas_call | solution.py:565
  35.7 0.1 collective-permute-start.9
  35.8 0.1 collective-permute-start.6
  35.8 1.3 %collective-permute-start.7 = (f32[24,512]{1,0:T(8,128)S(1)}, f32[24,512]{1,0:T(8,128)S(1)}, u32[]{:S(2)}, u32[]{:S(2)}) collective-permute-start(f32[24,512]{1,0:T(8,128)S(1)} %get-tuple-element.36), channel_id=1, source_target_pairs={{0,16},{8,24},{16,0},{24,8},{1,17},{9,25},{17,1},{25,9},{2,18},{10... | collective-permute-start | bytes 147464 | tf_op jit(solution)/shard_map/ppermute | solution.py:577
  37.1 2.5 %collective-permute-start.8 = (f32[24,512]{1,0:T(8,128)S(1)}, f32[24,512]{1,0:T(8,128)S(1)}, u32[]{:S(2)}, u32[]{:S(2)}) collective-permute-start(f32[24,512]{1,0:T(8,128)S(1)} %get-tuple-element.37), channel_id=1, source_target_pairs={{0,24},{8,0},{16,8},{24,16},{1,25},{9,1},{17,9},{25,17},{2,26},{10... | collective-permute-start | bytes 147464 | tf_op jit(solution)/shard_map/ppermute | solution.py:577
  39.6 0.0 collective-permute-done.9
  39.7 3.4 %collective-permute-start.12 = (f32[32,512]{1,0:T(8,128)S(1)}, f32[32,512]{1,0:T(8,128)S(1)}, u32[]{:S(2)}, u32[]{:S(2)}) collective-permute-start(f32[32,512]{1,0:T(8,128)S(1)} %constant_dynamic-update-slice_fusion.3.refs_0_), channel_id=1, source_target_pairs={{0,2},{1,3},{2,4},{3,5},{4,6},{5,7},{6,0},{7,1},{8,10},{9,11},{10,... | collective-permute-start | bytes 196616 | tf_op jit(solution)/shard_map/ppermute | solution.py:582
  43.1 2.2 %collective-permute-start.11 = (f32[32,512]{1,0:T(8,128)S(1)}, f32[32,512]{1,0:T(8,128)S(1)}, u32[]{:S(2)}, u32[]{:S(2)}) collective-permute-start(f32[32,512]{1,0:T(8,128)S(1)} %constant_dynamic-update-slice_fusion.3.refs_0_), channel_id=1, source_target_pairs={{0,4},{1,5},{2,6},{3,7},{4,0},{5,1},{6,2},{7,3},{8,12},{9,13},{10,... | collective-permute-start | bytes 196616 | tf_op jit(solution)/shard_map/ppermute | solution.py:582
  45.2 0.0 collective-permute-done.6.refs_3_
  45.2 2.7 %collective-permute-start.10 = (f32[32,512]{1,0:T(8,128)S(1)}, f32[32,512]{1,0:T(8,128)S(1)}, u32[]{:S(2)}, u32[]{:S(2)}) collective-permute-start(f32[32,512]{1,0:T(8,128)S(1)} %constant_dynamic-update-slice_fusion.3.refs_0_), channel_id=1, source_target_pairs={{0,6},{1,7},{2,0},{3,1},{4,2},{5,3},{6,4},{7,5},{8,14},{9,15},{10,... | collective-permute-start | bytes 196616 | tf_op jit(solution)/shard_map/ppermute | solution.py:582
  47.9 0.0 collective-permute-done.7.refs_4_
  48.0 0.0 collective-permute-done.8.refs_5_
  48.0 0.8 %final_cols.1.field = f32[16,512]{1,0:T(8,128)S(1)} custom-call(s32[2,6]{1,0:T(2,128)S(1)} %bitcast.9, f32[16,512]{1,0:T(8,128)S(1)} %get-tuple-element.22.weight, f32[16,512]{1,0:T(8,128)S(1)} %get-tuple-element.33.near, f32[17,4,512]{2,1,0:T(4,128)S(1)} %get-tuple-element.25.own_in.own_far, f32[16,512]{1,0:T(8,128)S(1)} %get-tuple-element.34.own_cols, ...), custom_call_target="tpu_custom_call" | custom-call | flops 1100000000 | bytes 65536 | tf_op jit(solution)/shard_map/final_cols/pallas_call | solution.py:583
  48.8 0.0 collective-permute-done.12.refs_3_
  48.8 0.0 collective-permute-done.11.refs_2_
  48.8 1.1 %collective-permute-done.10.refs_1_ = f32[32,512]{1,0:T(8,128)S(1)} collective-permute-done((f32[32,512]{1,0:T(8,128)S(1)}, f32[32,512]{1,0:T(8,128)S(1)}, u32[]{:S(2)}, u32[]{:S(2)}) %collective-permute-start.10) | collective-permute-done | bytes 65568 | tf_op jit(solution)/shard_map/ppermute | solution.py:582
  49.9 0.9 %final_rows.1 = f32[64,128]{1,0:T(8,128)} custom-call(f32[16,512]{1,0:T(8,128)S(1)} %get-tuple-element.22.weight, f32[16,512]{1,0:T(8,128)S(1)} %final_cols.1.field, f32[68,4,512]{2,1,0:T(4,128)S(1)} %constant_dynamic-update-slice_fusion.row0, f32[68,4,512]{2,1,0:T(4,128)S(1)} %collective-permute-done.4.row1, ...), custom_call_target="tpu_custom_call" | custom-call | flops 1100000000 | bytes 65536 | tf_op jit(solution)/shard_map/final_rows/pallas_call | solution.py:592
  (5 shorter events, 0.1 us)
Async XLA Ops:
  2.1 7.2 %collective-permute-start.2 = (f32[17,4,512]{2,1,0:T(4,128)S(1)}, f32[17,4,512]{2,1,0:T(4,128)S(1)}, u32[]{:S(2)}, u32[]{:S(2)}) collective-permute-start(f32[17,4,512]{2,1,0:T(4,128)S(1)} %get-tuple-element.25.own_in.own_far), channel_id=1, source_target_pairs={{0,4},{1,5},{2,6},{3,7},{4,0},{5,1},{6,2},{7,3},{8,12},{9,13},{10,... | collective-permute-start | bytes 417800 | tf_op jit(solution)/shard_map/ppermute | solution.py:465
  5.1 16.5 %collective-permute-start.1 = (f32[152,512]{1,0:T(8,128)S(1)}, f32[152,512]{1,0:T(8,128)S(1)}, u32[]{:S(2)}, u32[]{:S(2)}) collective-permute-start(f32[152,512]{1,0:T(8,128)S(1)} %get-tuple-element.24), channel_id=1, source_target_pairs={{0,16},{8,24},{16,0},{24,8},{1,17},{9,25},{17,1},{25,9},{2,18},{10... | collective-permute-start | bytes 933896 | tf_op jit(solution)/shard_map/ppermute | solution.py:465
  7.7 14.5 %collective-permute-start = (f32[152,512]{1,0:T(8,128)S(1)}, f32[152,512]{1,0:T(8,128)S(1)}, u32[]{:S(2)}, u32[]{:S(2)}) collective-permute-start(f32[152,512]{1,0:T(8,128)S(1)} %get-tuple-element.24), channel_id=1, source_target_pairs={{0,8},{8,0},{16,24},{24,16},{1,9},{9,1},{17,25},{25,17},{2,10},{10... | collective-permute-start | bytes 933896 | tf_op jit(solution)/shard_map/ppermute | solution.py:465
  9.4 1.6 %copy-start.1 = (s32[6,2]{0,1:T(2,128)S(1)}, s32[6,2]{0,1:T(2,128)}, u32[]{:S(2)}) copy-start(s32[6,2]{0,1:T(2,128)} %param.8) | copy-start | bytes 148
  9.4 7.6 %collective-permute-start.3 = (f32[34,4,512]{2,1,0:T(4,128)S(1)}, f32[34,4,512]{2,1,0:T(4,128)S(1)}, u32[]{:S(2)}, u32[]{:S(2)}) collective-permute-start(f32[34,4,512]{2,1,0:T(4,128)S(1)} %pad_maximum_fusion), channel_id=1, source_target_pairs={{0,2},{1,3},{2,0},{3,1},{4,6},{5,7},{6,4},{7,5},{8,10},{9,11},{10,... | collective-permute-start | bytes 835592 | tf_op jit(solution)/shard_map/ppermute | solution.py:465
  17.0 6.1 %copy-start = (s32[16,2]{0,1:T(2,128)S(1)}, s32[16,2]{0,1:T(2,128)}, u32[]{:S(2)}) copy-start(s32[16,2]{0,1:T(2,128)} %param.9) | copy-start | bytes 388
  17.0 6.1 %collective-permute-start.4 = (f32[68,4,512]{2,1,0:T(4,128)S(1)}, f32[68,4,512]{2,1,0:T(4,128)S(1)}, u32[]{:S(2)}, u32[]{:S(2)}) collective-permute-start(f32[68,4,512]{2,1,0:T(4,128)S(1)} %constant_dynamic-update-slice_fusion.row0), channel_id=1, source_target_pairs={{0,1},{1,0},{2,3},{3,2},{4,5},{5,4},{6,7},{7,6},{8,9},{9,8},{10,11... | collective-permute-start | bytes 1671176 | tf_op jit(solution)/shard_map/ppermute | solution.py:465
  21.6 8.1 %collective-permute-start.5 = (f32[152,512]{1,0:T(8,128)S(1)}, f32[152,512]{1,0:T(8,128)S(1)}, u32[]{:S(2)}, u32[]{:S(2)}) collective-permute-start(f32[152,512]{1,0:T(8,128)S(1)} %collective-permute-done.1.refs_1_), channel_id=1, source_target_pairs={{0,8},{8,0},{16,24},{24,16},{1,9},{9,1},{17,25},{25,17},{2,10},{10... | collective-permute-start | bytes 933896 | tf_op jit(solution)/shard_map/ppermute | solution.py:465
  35.7 4.0 %collective-permute-start.9 = (f32[16,512]{1,0:T(8,128)S(1)}, f32[16,512]{1,0:T(8,128)S(1)}, u32[]{:S(2)}, u32[]{:S(2)}) collective-permute-start(f32[16,512]{1,0:T(8,128)S(1)} %get-tuple-element.38), channel_id=1, source_target_pairs={{0,1},{1,0},{2,3},{3,2},{4,5},{5,4},{6,7},{7,6},{8,9},{9,8},{10,11... | collective-permute-start | bytes 98312 | tf_op jit(solution)/shard_map/ppermute | solution.py:465
  35.8 9.5 %collective-permute-start.6 = (f32[24,512]{1,0:T(8,128)S(1)}, f32[24,512]{1,0:T(8,128)S(1)}, u32[]{:S(2)}, u32[]{:S(2)}) collective-permute-start(f32[24,512]{1,0:T(8,128)S(1)} %get-tuple-element.35), channel_id=1, source_target_pairs={{0,8},{8,16},{16,24},{24,0},{1,9},{9,17},{17,25},{25,1},{2,10},{10... | collective-permute-start | bytes 147464 | tf_op jit(solution)/shard_map/ppermute | solution.py:577
  35.8 12.1 %collective-permute-start.7 = (f32[24,512]{1,0:T(8,128)S(1)}, f32[24,512]{1,0:T(8,128)S(1)}, u32[]{:S(2)}, u32[]{:S(2)}) collective-permute-start(f32[24,512]{1,0:T(8,128)S(1)} %get-tuple-element.36), channel_id=1, source_target_pairs={{0,16},{8,24},{16,0},{24,8},{1,17},{9,25},{17,1},{25,9},{2,18},{10... | collective-permute-start | bytes 147464 | tf_op jit(solution)/shard_map/ppermute | solution.py:577
  37.1 10.8 %collective-permute-start.8 = (f32[24,512]{1,0:T(8,128)S(1)}, f32[24,512]{1,0:T(8,128)S(1)}, u32[]{:S(2)}, u32[]{:S(2)}) collective-permute-start(f32[24,512]{1,0:T(8,128)S(1)} %get-tuple-element.37), channel_id=1, source_target_pairs={{0,24},{8,0},{16,8},{24,16},{1,25},{9,1},{17,9},{25,17},{2,26},{10... | collective-permute-start | bytes 147464 | tf_op jit(solution)/shard_map/ppermute | solution.py:577
  39.7 9.1 %collective-permute-start.12 = (f32[32,512]{1,0:T(8,128)S(1)}, f32[32,512]{1,0:T(8,128)S(1)}, u32[]{:S(2)}, u32[]{:S(2)}) collective-permute-start(f32[32,512]{1,0:T(8,128)S(1)} %constant_dynamic-update-slice_fusion.3.refs_0_), channel_id=1, source_target_pairs={{0,2},{1,3},{2,4},{3,5},{4,6},{5,7},{6,0},{7,1},{8,10},{9,11},{10,... | collective-permute-start | bytes 196616 | tf_op jit(solution)/shard_map/ppermute | solution.py:582
  43.1 5.7 %collective-permute-start.11 = (f32[32,512]{1,0:T(8,128)S(1)}, f32[32,512]{1,0:T(8,128)S(1)}, u32[]{:S(2)}, u32[]{:S(2)}) collective-permute-start(f32[32,512]{1,0:T(8,128)S(1)} %constant_dynamic-update-slice_fusion.3.refs_0_), channel_id=1, source_target_pairs={{0,4},{1,5},{2,6},{3,7},{4,0},{5,1},{6,2},{7,3},{8,12},{9,13},{10,... | collective-permute-start | bytes 196616 | tf_op jit(solution)/shard_map/ppermute | solution.py:582
  45.2 4.6 %collective-permute-start.10 = (f32[32,512]{1,0:T(8,128)S(1)}, f32[32,512]{1,0:T(8,128)S(1)}, u32[]{:S(2)}, u32[]{:S(2)}) collective-permute-start(f32[32,512]{1,0:T(8,128)S(1)} %constant_dynamic-update-slice_fusion.3.refs_0_), channel_id=1, source_target_pairs={{0,6},{1,7},{2,0},{3,1},{4,2},{5,3},{6,4},{7,5},{8,14},{9,15},{10,... | collective-permute-start | bytes 196616 | tf_op jit(solution)/shard_map/ppermute | solution.py:582

commit v2 on v1

--- a/solution.py
+++ b/solution.py
@@ -15,6 +15,7 @@
 HALF = 512
 QUARTERS = 4
 SLOTS = 5
+OWN_FIRST = 2
 NEAR_SCRATCH = 4 * [None]
 GROUP = 16
 CHUNK = 512
@@ -279,10 +280,11 @@
     my_row = lax.axis_index("row")
     field[...] = jnp.zeros_like(field)
 
-    def step(s, _):
+    def step(s, n):
         ka, kb = lax.rem(pairs[0, s], blocks), pairs[1, s] - my_row * blocks
-
-        @pl.when((kb >= 0) & (kb < blocks))
+        own = (kb >= 0) & (kb < blocks)
+
+        @pl.when(own & (n < OWN_FIRST))
         def _():
             left, right = points(near_ref[ka, 0:body, :]), points(near_ref[kb, 0:body, :])
             dens_i, dens_j = near_ref[ka, body : body + 1, :], near_ref[kb, body : body + 1, :]
@@ -290,12 +292,12 @@
             field[pl.ds(ka, 1), :] += rows
             field[pl.ds(kb, 1), :] += cols * jnp.where(ka == kb, 0.0, 1.0)
 
-        return 0
-
-    lax.fori_loop(0, count[0], step, 0)
-
-
-def near_tiles(meanwhile, near_ref, got, field, put, right_buf, tags, sems, *bufs):
+        return n + own.astype(jnp.int32)
+
+    lax.fori_loop(0, count[0], step, jnp.int32(0))
+
+
+def near_tiles(meanwhile, near_ref, got, field, put, right_buf, tags, sems, *bufs, own=None):
     blocks, depth, _ = near_ref.shape
     body = depth - 8
     base = near_lines(SLOTS, body // 4)
@@ -310,10 +312,25 @@
 
     def step(i, _):
         way, t = lax.div(i, SLOTS), lax.rem(i, SLOTS)
-        kb = tags[way, 3, t].astype(jnp.int32) - my_row * blocks
+        kb = tags[jnp.minimum(way, len(got) - 1), 3, t].astype(jnp.int32) - my_row * blocks
+        if own is not None:
+            pairs, count = own
+            before = jnp.int32(0)
+            for s in range(SLOTS + 1):
+                inside = (pairs[1, s] >= my_row * blocks) & (pairs[1, s] < (my_row + 1) * blocks)
+                before = before + jnp.where(inside & (s <= t), 1, 0)
+            left_over = (t + 1 < count[0]) & (before >= OWN_FIRST)
+            own_kb = jnp.where(left_over, pairs[1, t + 1] - my_row * blocks, -1)
+            kb = jnp.where(way == len(got), own_kb, kb)
 
         @pl.when((kb >= 0) & (kb < blocks))
         def _():
+            if own is not None:
+
+                @pl.when(way == len(got))
+                def _():
+                    right_buf[...] = near_ref[lax.rem(own[0][0, t + 1], blocks)]
+
             for d, other in enumerate(got):
 
                 @pl.when(way == d)
@@ -330,13 +347,19 @@
             rows, cols = near_tile(left, dens_i, right, dens_j, *bufs)
             field[pl.ds(kb, 1), :] += rows
             put(way, t, cols)
+            if own is not None:
+                ka = lax.rem(own[0][0, t + 1], blocks)
+
+                @pl.when(way == len(got))
+                def _():
+                    field[pl.ds(ka, 1), :] += cols * jnp.where(ka == kb, 0.0, 1.0)
 
         return 0
 
-    lax.fori_loop(0, len(got) * SLOTS, step, 0)
-
-
-def direct_kernel(near_ref, start, *refs, ways):
+    lax.fori_loop(0, (len(got) + (own is not None)) * SLOTS, step, 0)
+
+
+def direct_kernel(pairs, count, near_ref, start, *refs, ways):
     got, (field, *backs), scratch = refs[:ways], refs[ways : 2 * ways + 1], refs[2 * ways + 1 :]
 
     def clear():
@@ -351,7 +374,7 @@
             def _():
                 back[pl.ds(t, 1), :] = result
 
-    near_tiles(clear, near_ref, got, field, put, *scratch)
+    near_tiles(clear, near_ref, got, field, put, *scratch, own=(pairs, count))
 
 
 def far_kernel(pairs, count, row0, row1, own_in, *refs, direct, base):
@@ -545,13 +568,13 @@
     field, *backs = pl.pallas_call(
         functools.partial(direct_kernel, ways=len(direct)),
         out_shape=[f32(blocks, BLK)] + [f32(8, BLK)] * len(direct),
-        in_specs=[VMEM] * (2 + len(direct)),
+        in_specs=[SMEM, SMEM] + [VMEM] * (2 + len(direct)),
         out_specs=[VMEM] * (len(direct) + 1),
         scratch_shapes=near_scratch(len(direct)),
         compiler_params=PARAMS,
         cost_estimate=cost(30.0),
         name="near_direct",
-    )(near_own, near0, *[got[d - 1] for d in direct])
+    )(near_pairs, near_count, near_own, near0, *[got[d - 1] for d in direct])
     far_rows, far_cols = pl.pallas_call(
         functools.partial(far_kernel, direct=direct, base=base),
         out_shape=[f32(nfar, BLK)] * 2,

time: 50.8 us -> 50.3 us (level)
  Pallas kernels: 16.7 us -> 11.9 us
  starting transfers between devices: 21.6 us -> 24.7 us
  waiting for transfers between devices: 10.8 us -> 11.9 us
    ppermute x7, starting transfers between devices: 9.46 us -> 15.1 us  [swap(): return lax.ppermute(x, axis, [(i, i ^ d) for i in range(n)])]
    ppermute x3, starting transfers between devices: 8.29 us -> 3.43 us  [body(): lax.ppermute(both, 'col', [(i, (i - k) % n_col) for i in range(n_col)])]
    pallas_call x1, Pallas kernels: 5.9 us -> 1.29 us  [body(): pl.pallas_call(functools.partial(late_kernel, n_row=n_row, direct=direct,...]
    ppermute x3, starting transfers between devices: 3.88 us -> 6.2 us  [body(): lax.ppermute(x, 'row', [(i, (i + k + 1) % n_row) for i in range(n_row)])]
    pallas_call x1, Pallas kernels: 3.27 us -> 2.22 us  [body(): pl.pallas_call(functools.partial(far_kernel, direct=direct, base=base), o...]
    ppermute x3, waiting for transfers between devices: 1.07 us -> 1.97 us  [body(): lax.ppermute(both, 'col', [(i, (i - k) % n_col) for i in range(n_col)])]
    pallas_call x1, Pallas kernels: 0.95 us -> 1.82 us  [body(): pl.pallas_call(functools.partial(direct_kernel, ways=len(direct)), out_sh...]
  transfers between devices with their start and end apart: 13 -> 13, of which waited for: 4 -> 5; matrix products, arithmetic and copies ran while one was open for 0% -> 0% of each run, Pallas kernels for 17% -> 17%
where the time goes in v2:
time: 50.3 us; the launch traced here: 50.1 us
  starting transfers between devices  24.7 us (49%)
  Pallas kernels  11.9 us (24%)
  waiting for transfers between devices  11.9 us (24%)
  between operations  1.41 us (3%)
    ppermute x7, starting transfers between devices, swap(): return lax.ppermute(x, axis, [(i, i ^ d) for i in range(n)])  15.1 us
    ppermute x7, waiting for transfers between devices, swap(): return lax.ppermute(x, axis, [(i, i ^ d) for i in range(n)])  9.9 us
    ppermute x3, starting transfers between devices, body(): lax.ppermute(x, 'row', [(i, (i + k + 1) % n_row) for i in range(n_row)])  6.2 us
    pallas_call x1, Pallas kernels, body(): pl.pallas_call(near_own_kernel, out_shape=f32(blocks, BLK), in_specs=[SME...  3.47 us
    ppermute x3, starting transfers between devices, body(): lax.ppermute(both, 'col', [(i, (i - k) % n_col) for i in range(n_col)])  3.43 us
    pallas_call x1, Pallas kernels, body(): pl.pallas_call(functools.partial(far_kernel, direct=direct, base=base), o...  2.22 us
    ppermute x3, waiting for transfers between devices, body(): lax.ppermute(both, 'col', [(i, (i - k) % n_col) for i in range(n_col)])  1.97 us
    pallas_call x1, Pallas kernels, body(): pl.pallas_call(functools.partial(direct_kernel, ways=len(direct)), out_sh...  1.82 us
  transfers between devices with their start and end apart: 13, of which 5 were waited for; matrix products, arithmetic and copies ran while one was open for 0% of the time, Pallas kernels for 17%

profile of v2, /device:TPU:0, one launch (start us, length us, event | category | flops | bytes accessed | tf_op | source)
XLA Modules:
  0.0 50.1 jit_solution(6082153100099261264)
XLA Ops:
  0.7 1.4 %prep.1 = (f32[152,512]{1,0:T(8,128)S(1)}, f32[17,4,512]{2,1,0:T(4,128)S(1)}, f32[16,24,512]{2,1,0:T(8,128)S(1)}, f32[16,512]{1,0:T(8,128)S(1)}) custom-call(s32[2,6]{1,0:T(2,128)} %bitcast.7, s32[1]{0:T(128)S(6)} %copy.10.count, s32[2,16]{1,0:T(2,128)} %bitcast.4, f32[4,4,8192]{2,1,0:T(4,128)} %pts_hbm.1, f32[64,128]{1,0:T(8,128)} %bitcast.11), custom_call_target="tpu_custom_call" | custom-call | flops 1320000000 | bytes 65536 | tf_op jit(solution)/shard_map/prep/pallas_call | solution.py:505
  2.1 3.0 %collective-permute-start.2 = (f32[17,4,512]{2,1,0:T(4,128)S(1)}, f32[17,4,512]{2,1,0:T(4,128)S(1)}, u32[]{:S(2)}, u32[]{:S(2)}) collective-permute-start(f32[17,4,512]{2,1,0:T(4,128)S(1)} %get-tuple-element.25.own_in.own_far), channel_id=1, source_target_pairs={{0,4},{1,5},{2,6},{3,7},{4,0},{5,1},{6,2},{7,3},{8,12},{9,13},{10,... | collective-permute-start | bytes 417800 | tf_op jit(solution)/shard_map/ppermute | solution.py:488
  5.1 2.6 %collective-permute-start.1 = (f32[152,512]{1,0:T(8,128)S(1)}, f32[152,512]{1,0:T(8,128)S(1)}, u32[]{:S(2)}, u32[]{:S(2)}) collective-permute-start(f32[152,512]{1,0:T(8,128)S(1)} %get-tuple-element.24), channel_id=1, source_target_pairs={{0,16},{8,24},{16,0},{24,8},{1,17},{9,25},{17,1},{25,9},{2,18},{10... | collective-permute-start | bytes 933896 | tf_op jit(solution)/shard_map/ppermute | solution.py:488
  7.7 1.6 %collective-permute-start = (f32[152,512]{1,0:T(8,128)S(1)}, f32[152,512]{1,0:T(8,128)S(1)}, u32[]{:S(2)}, u32[]{:S(2)}) collective-permute-start(f32[152,512]{1,0:T(8,128)S(1)} %get-tuple-element.24), channel_id=1, source_target_pairs={{0,8},{8,0},{16,24},{24,16},{1,9},{9,1},{17,25},{25,17},{2,10},{10... | collective-permute-start | bytes 933896 | tf_op jit(solution)/shard_map/ppermute | solution.py:488
  9.3 0.0 collective-permute-done.2
  9.3 0.1 pad_maximum_fusion
  9.4 0.0 copy-start.1
  9.4 1.6 %collective-permute-start.3 = (f32[34,4,512]{2,1,0:T(4,128)S(1)}, f32[34,4,512]{2,1,0:T(4,128)S(1)}, u32[]{:S(2)}, u32[]{:S(2)}) collective-permute-start(f32[34,4,512]{2,1,0:T(4,128)S(1)} %pad_maximum_fusion), channel_id=1, source_target_pairs={{0,2},{1,3},{2,0},{3,1},{4,6},{5,7},{6,4},{7,5},{8,10},{9,11},{10,... | collective-permute-start | bytes 835592 | tf_op jit(solution)/shard_map/ppermute | solution.py:488
  10.9 0.0 copy-done.1
  10.9 3.5 %near_own.1.start = f32[16,512]{1,0:T(8,128)S(1)} custom-call(s32[2,6]{1,0:T(2,128)S(1)} %bitcast.8, s32[1]{0:T(128)S(6)} %copy.10.count, f32[16,24,512]{2,1,0:T(8,128)S(1)} %get-tuple-element.23.near_ref), custom_call_target="tpu_custom_call" | custom-call | flops 5500000256 | bytes 65536 | tf_op jit(solution)/shard_map/near_own/pallas_call | solution.py:542
  15.1 1.9 %collective-permute-done.3 = f32[34,4,512]{2,1,0:T(4,128)S(1)} collective-permute-done((f32[34,4,512]{2,1,0:T(4,128)S(1)}, f32[34,4,512]{2,1,0:T(4,128)S(1)}, u32[]{:S(2)}, u32[]{:S(2)}) %collective-permute-start.3) | collective-permute-done | bytes 278560 | tf_op jit(solution)/shard_map/ppermute | solution.py:488
  17.0 0.0 copy-start
  17.0 0.1 collective-permute-start.4
  17.1 4.5 %collective-permute-done.1.refs_1_ = f32[152,512]{1,0:T(8,128)S(1)} collective-permute-done((f32[152,512]{1,0:T(8,128)S(1)}, f32[152,512]{1,0:T(8,128)S(1)}, u32[]{:S(2)}, u32[]{:S(2)}) %collective-permute-start.1) | collective-permute-done | bytes 311328 | tf_op jit(solution)/shard_map/ppermute | solution.py:488
  21.6 0.6 %collective-permute-start.5 = (f32[152,512]{1,0:T(8,128)S(1)}, f32[152,512]{1,0:T(8,128)S(1)}, u32[]{:S(2)}, u32[]{:S(2)}) collective-permute-start(f32[152,512]{1,0:T(8,128)S(1)} %collective-permute-done.1.refs_1_), channel_id=1, source_target_pairs={{0,8},{8,0},{16,24},{24,16},{1,9},{9,1},{17,25},{25,17},{2,10},{10... | collective-permute-start | bytes 933896 | tf_op jit(solution)/shard_map/ppermute | solution.py:488
  22.2 0.0 collective-permute-done.refs_0_
  22.2 1.8 %near_direct.1 = (f32[16,512]{1,0:T(8,128)S(1)}, f32[8,512]{1,0:T(8,128)S(1)}, f32[8,512]{1,0:T(8,128)S(1)}) custom-call(s32[2,6]{1,0:T(2,128)S(1)} %bitcast.9, s32[1]{0:T(128)S(6)} %copy.10.count, f32[16,24,512]{2,1,0:T(8,128)S(1)} %get-tuple-element.23.near_ref, f32[16,512]{1,0:T(8,128)S(1)} %near_own.1.start, ...), custom_call_target="tpu_custom_call" | custom-call | flops 32999999488 | bytes 65536 | tf_op jit(solution)/shard_map/near_direct/pallas_call | solution.py:568
  24.0 0.0 collective-permute-done.4.row1
  24.0 0.0 copy-done
  24.0 2.2 %far_direct.1 = (f32[16,512]{1,0:T(8,128)S(1)}, f32[16,512]{1,0:T(8,128)S(1)}) custom-call(s32[2,16]{1,0:T(2,128)S(1)} %bitcast.5, s32[1]{0:T(128)S(6)} %copy.11.count, f32[68,4,512]{2,1,0:T(4,128)S(1)} %constant_dynamic-update-slice_fusion.row0, f32[68,4,512]{2,1,0:T(4,128)S(1)} %collective-permute-done.4.row1, ...), custom_call_target="tpu_custom_call" | custom-call | flops 3300000000 | bytes 65536 | tf_op jit(solution)/shard_map/far_direct/pallas_call | solution.py:578
  26.3 3.5 %collective-permute-done.5.refs_0_.refs_2_ = f32[152,512]{1,0:T(8,128)S(1)} collective-permute-done((f32[152,512]{1,0:T(8,128)S(1)}, f32[152,512]{1,0:T(8,128)S(1)}, u32[]{:S(2)}, u32[]{:S(2)}) %collective-permute-start.5) | collective-permute-done | bytes 311328 | tf_op jit(solution)/shard_map/ppermute | solution.py:488
  29.8 1.3 %late.1 = (f32[16,512]{1,0:T(8,128)S(1)}, f32[16,512]{1,0:T(8,128)S(1)}, f32[16,512]{1,0:T(8,128)S(1)}, f32[24,512]{1,0:T(8,128)S(1)}, f32[24,512]{1,0:T(8,128)S(1)}, /*index=5*/f32[24,512]{1,0:T(8,128)S(1)}) custom-call(s32[2,16]{1,0:T(2,128)S(1)} %bitcast.6, s32[1]{0:T(128)S(6)} %copy.11.count, f32[16,24,512]{2,1,0:T(8,128)S(1)} %get-tuple-element.23.near_ref, ...), custom_call_target="tpu_custom_call" | custom-call | flops 8800000000 | bytes 65536 | tf_op jit(solution)/shard_map/late/pallas_call | solution.py:588
  31.1 5.7 %collective-permute-start.9 = (f32[16,512]{1,0:T(8,128)S(1)}, f32[16,512]{1,0:T(8,128)S(1)}, u32[]{:S(2)}, u32[]{:S(2)}) collective-permute-start(f32[16,512]{1,0:T(8,128)S(1)} %get-tuple-element.38), channel_id=1, source_target_pairs={{0,1},{1,0},{2,3},{3,2},{4,5},{5,4},{6,7},{7,6},{8,9},{9,8},{10,11... | collective-permute-start | bytes 98312 | tf_op jit(solution)/shard_map/ppermute | solution.py:488
  36.8 0.0 collective-permute-start.6
  36.8 3.3 %collective-permute-start.7 = (f32[24,512]{1,0:T(8,128)S(1)}, f32[24,512]{1,0:T(8,128)S(1)}, u32[]{:S(2)}, u32[]{:S(2)}) collective-permute-start(f32[24,512]{1,0:T(8,128)S(1)} %get-tuple-element.36), channel_id=1, source_target_pairs={{0,16},{8,24},{16,0},{24,8},{1,17},{9,25},{17,1},{25,9},{2,18},{10... | collective-permute-start | bytes 147464 | tf_op jit(solution)/shard_map/ppermute | solution.py:600
  40.1 2.9 %collective-permute-start.8 = (f32[24,512]{1,0:T(8,128)S(1)}, f32[24,512]{1,0:T(8,128)S(1)}, u32[]{:S(2)}, u32[]{:S(2)}) collective-permute-start(f32[24,512]{1,0:T(8,128)S(1)} %get-tuple-element.37), channel_id=1, source_target_pairs={{0,24},{8,0},{16,8},{24,16},{1,25},{9,1},{17,9},{25,17},{2,26},{10... | collective-permute-start | bytes 147464 | tf_op jit(solution)/shard_map/ppermute | solution.py:600
  43.0 0.0 collective-permute-done.9
  43.0 1.9 %collective-permute-start.12 = (f32[32,512]{1,0:T(8,128)S(1)}, f32[32,512]{1,0:T(8,128)S(1)}, u32[]{:S(2)}, u32[]{:S(2)}) collective-permute-start(f32[32,512]{1,0:T(8,128)S(1)} %constant_dynamic-update-slice_fusion.3.refs_0_), channel_id=1, source_target_pairs={{0,2},{1,3},{2,4},{3,5},{4,6},{5,7},{6,0},{7,1},{8,10},{9,11},{10,... | collective-permute-start | bytes 196616 | tf_op jit(solution)/shard_map/ppermute | solution.py:605
  44.9 0.0 collective-permute-start.11
  44.9 0.0 collective-permute-done.6.refs_3_
  44.9 1.5 %collective-permute-start.10 = (f32[32,512]{1,0:T(8,128)S(1)}, f32[32,512]{1,0:T(8,128)S(1)}, u32[]{:S(2)}, u32[]{:S(2)}) collective-permute-start(f32[32,512]{1,0:T(8,128)S(1)} %constant_dynamic-update-slice_fusion.3.refs_0_), channel_id=1, source_target_pairs={{0,6},{1,7},{2,0},{3,1},{4,2},{5,3},{6,4},{7,5},{8,14},{9,15},{10,... | collective-permute-start | bytes 196616 | tf_op jit(solution)/shard_map/ppermute | solution.py:605
  46.4 0.0 collective-permute-done.7.refs_4_
  46.4 0.0 collective-permute-done.8.refs_5_
  46.4 0.8 %final_cols.1.field = f32[16,512]{1,0:T(8,128)S(1)} custom-call(s32[2,6]{1,0:T(2,128)S(1)} %bitcast.10, f32[16,512]{1,0:T(8,128)S(1)} %get-tuple-element.22.weight, f32[16,512]{1,0:T(8,128)S(1)} %get-tuple-element.33.near, f32[17,4,512]{2,1,0:T(4,128)S(1)} %get-tuple-element.25.own_in.own_far, f32[16,512]{1,0:T(8,128)S(1)} %get-tuple-element.34.own_cols, ...), custom_call_target="tpu_custom_call" | custom-call | flops 1100000000 | bytes 65536 | tf_op jit(solution)/shard_map/final_cols/pallas_call | solution.py:606
  47.2 1.0 %collective-permute-done.12.refs_3_ = f32[32,512]{1,0:T(8,128)S(1)} collective-permute-done((f32[32,512]{1,0:T(8,128)S(1)}, f32[32,512]{1,0:T(8,128)S(1)}, u32[]{:S(2)}, u32[]{:S(2)}) %collective-permute-start.12) | collective-permute-done | bytes 65568 | tf_op jit(solution)/shard_map/ppermute | solution.py:605
  48.3 0.9 %collective-permute-done.11.refs_2_ = f32[32,512]{1,0:T(8,128)S(1)} collective-permute-done((f32[32,512]{1,0:T(8,128)S(1)}, f32[32,512]{1,0:T(8,128)S(1)}, u32[]{:S(2)}, u32[]{:S(2)}) %collective-permute-start.11) | collective-permute-done | bytes 65568 | tf_op jit(solution)/shard_map/ppermute | solution.py:605
  49.2 0.0 collective-permute-done.10.refs_1_
  49.2 0.9 %final_rows.1 = f32[64,128]{1,0:T(8,128)} custom-call(f32[16,512]{1,0:T(8,128)S(1)} %get-tuple-element.22.weight, f32[16,512]{1,0:T(8,128)S(1)} %final_cols.1.field, f32[68,4,512]{2,1,0:T(4,128)S(1)} %constant_dynamic-update-slice_fusion.row0, f32[68,4,512]{2,1,0:T(4,128)S(1)} %collective-permute-done.4.row1, ...), custom_call_target="tpu_custom_call" | custom-call | flops 1100000000 | bytes 65536 | tf_op jit(solution)/shard_map/final_rows/pallas_call | solution.py:615
  (5 shorter events, 0.1 us)
Async XLA Ops:
  2.1 7.2 %collective-permute-start.2 = (f32[17,4,512]{2,1,0:T(4,128)S(1)}, f32[17,4,512]{2,1,0:T(4,128)S(1)}, u32[]{:S(2)}, u32[]{:S(2)}) collective-permute-start(f32[17,4,512]{2,1,0:T(4,128)S(1)} %get-tuple-element.25.own_in.own_far), channel_id=1, source_target_pairs={{0,4},{1,5},{2,6},{3,7},{4,0},{5,1},{6,2},{7,3},{8,12},{9,13},{10,... | collective-permute-start | bytes 417800 | tf_op jit(solution)/shard_map/ppermute | solution.py:488
  5.1 16.5 %collective-permute-start.1 = (f32[152,512]{1,0:T(8,128)S(1)}, f32[152,512]{1,0:T(8,128)S(1)}, u32[]{:S(2)}, u32[]{:S(2)}) collective-permute-start(f32[152,512]{1,0:T(8,128)S(1)} %get-tuple-element.24), channel_id=1, source_target_pairs={{0,16},{8,24},{16,0},{24,8},{1,17},{9,25},{17,1},{25,9},{2,18},{10... | collective-permute-start | bytes 933896 | tf_op jit(solution)/shard_map/ppermute | solution.py:488
  7.7 14.5 %collective-permute-start = (f32[152,512]{1,0:T(8,128)S(1)}, f32[152,512]{1,0:T(8,128)S(1)}, u32[]{:S(2)}, u32[]{:S(2)}) collective-permute-start(f32[152,512]{1,0:T(8,128)S(1)} %get-tuple-element.24), channel_id=1, source_target_pairs={{0,8},{8,0},{16,24},{24,16},{1,9},{9,1},{17,25},{25,17},{2,10},{10... | collective-permute-start | bytes 933896 | tf_op jit(solution)/shard_map/ppermute | solution.py:488
  9.4 1.6 %copy-start.1 = (s32[6,2]{0,1:T(2,128)S(1)}, s32[6,2]{0,1:T(2,128)}, u32[]{:S(2)}) copy-start(s32[6,2]{0,1:T(2,128)} %param.8) | copy-start | bytes 148
  9.4 7.6 %collective-permute-start.3 = (f32[34,4,512]{2,1,0:T(4,128)S(1)}, f32[34,4,512]{2,1,0:T(4,128)S(1)}, u32[]{:S(2)}, u32[]{:S(2)}) collective-permute-start(f32[34,4,512]{2,1,0:T(4,128)S(1)} %pad_maximum_fusion), channel_id=1, source_target_pairs={{0,2},{1,3},{2,0},{3,1},{4,6},{5,7},{6,4},{7,5},{8,10},{9,11},{10,... | collective-permute-start | bytes 835592 | tf_op jit(solution)/shard_map/ppermute | solution.py:488
  17.0 7.0 %copy-start = (s32[16,2]{0,1:T(2,128)S(1)}, s32[16,2]{0,1:T(2,128)}, u32[]{:S(2)}) copy-start(s32[16,2]{0,1:T(2,128)} %param.9) | copy-start | bytes 388
  17.0 7.0 %collective-permute-start.4 = (f32[68,4,512]{2,1,0:T(4,128)S(1)}, f32[68,4,512]{2,1,0:T(4,128)S(1)}, u32[]{:S(2)}, u32[]{:S(2)}) collective-permute-start(f32[68,4,512]{2,1,0:T(4,128)S(1)} %constant_dynamic-update-slice_fusion.row0), channel_id=1, source_target_pairs={{0,1},{1,0},{2,3},{3,2},{4,5},{5,4},{6,7},{7,6},{8,9},{9,8},{10,11... | collective-permute-start | bytes 1671176 | tf_op jit(solution)/shard_map/ppermute | solution.py:488
  21.6 8.1 %collective-permute-start.5 = (f32[152,512]{1,0:T(8,128)S(1)}, f32[152,512]{1,0:T(8,128)S(1)}, u32[]{:S(2)}, u32[]{:S(2)}) collective-permute-start(f32[152,512]{1,0:T(8,128)S(1)} %collective-permute-done.1.refs_1_), channel_id=1, source_target_pairs={{0,8},{8,0},{16,24},{24,16},{1,9},{9,1},{17,25},{25,17},{2,10},{10... | collective-permute-start | bytes 933896 | tf_op jit(solution)/shard_map/ppermute | solution.py:488
  31.1 11.9 %collective-permute-start.9 = (f32[16,512]{1,0:T(8,128)S(1)}, f32[16,512]{1,0:T(8,128)S(1)}, u32[]{:S(2)}, u32[]{:S(2)}) collective-permute-start(f32[16,512]{1,0:T(8,128)S(1)} %get-tuple-element.38), channel_id=1, source_target_pairs={{0,1},{1,0},{2,3},{3,2},{4,5},{5,4},{6,7},{7,6},{8,9},{9,8},{10,11... | collective-permute-start | bytes 98312 | tf_op jit(solution)/shard_map/ppermute | solution.py:488
  36.8 8.1 %collective-permute-start.6 = (f32[24,512]{1,0:T(8,128)S(1)}, f32[24,512]{1,0:T(8,128)S(1)}, u32[]{:S(2)}, u32[]{:S(2)}) collective-permute-start(f32[24,512]{1,0:T(8,128)S(1)} %get-tuple-element.35), channel_id=1, source_target_pairs={{0,8},{8,16},{16,24},{24,0},{1,9},{9,17},{17,25},{25,1},{2,10},{10... | collective-permute-start | bytes 147464 | tf_op jit(solution)/shard_map/ppermute | solution.py:600
  36.8 9.6 %collective-permute-start.7 = (f32[24,512]{1,0:T(8,128)S(1)}, f32[24,512]{1,0:T(8,128)S(1)}, u32[]{:S(2)}, u32[]{:S(2)}) collective-permute-start(f32[24,512]{1,0:T(8,128)S(1)} %get-tuple-element.36), channel_id=1, source_target_pairs={{0,16},{8,24},{16,0},{24,8},{1,17},{9,25},{17,1},{25,9},{2,18},{10... | collective-permute-start | bytes 147464 | tf_op jit(solution)/shard_map/ppermute | solution.py:600
  40.1 6.4 %collective-permute-start.8 = (f32[24,512]{1,0:T(8,128)S(1)}, f32[24,512]{1,0:T(8,128)S(1)}, u32[]{:S(2)}, u32[]{:S(2)}) collective-permute-start(f32[24,512]{1,0:T(8,128)S(1)} %get-tuple-element.37), channel_id=1, source_target_pairs={{0,24},{8,0},{16,8},{24,16},{1,25},{9,1},{17,9},{25,17},{2,26},{10... | collective-permute-start | bytes 147464 | tf_op jit(solution)/shard_map/ppermute | solution.py:600
  43.0 5.3 %collective-permute-start.12 = (f32[32,512]{1,0:T(8,128)S(1)}, f32[32,512]{1,0:T(8,128)S(1)}, u32[]{:S(2)}, u32[]{:S(2)}) collective-permute-start(f32[32,512]{1,0:T(8,128)S(1)} %constant_dynamic-update-slice_fusion.3.refs_0_), channel_id=1, source_target_pairs={{0,2},{1,3},{2,4},{3,5},{4,6},{5,7},{6,0},{7,1},{8,10},{9,11},{10,... | collective-permute-start | bytes 196616 | tf_op jit(solution)/shard_map/ppermute | solution.py:605
  44.9 4.3 %collective-permute-start.11 = (f32[32,512]{1,0:T(8,128)S(1)}, f32[32,512]{1,0:T(8,128)S(1)}, u32[]{:S(2)}, u32[]{:S(2)}) collective-permute-start(f32[32,512]{1,0:T(8,128)S(1)} %constant_dynamic-update-slice_fusion.3.refs_0_), channel_id=1, source_target_pairs={{0,4},{1,5},{2,6},{3,7},{4,0},{5,1},{6,2},{7,3},{8,12},{9,13},{10,... | collective-permute-start | bytes 196616 | tf_op jit(solution)/shard_map/ppermute | solution.py:605
  44.9 4.3 %collective-permute-start.10 = (f32[32,512]{1,0:T(8,128)S(1)}, f32[32,512]{1,0:T(8,128)S(1)}, u32[]{:S(2)}, u32[]{:S(2)}) collective-permute-start(f32[32,512]{1,0:T(8,128)S(1)} %constant_dynamic-update-slice_fusion.3.refs_0_), channel_id=1, source_target_pairs={{0,6},{1,7},{2,0},{3,1},{4,2},{5,3},{6,4},{7,5},{8,14},{9,15},{10,... | collective-permute-start | bytes 196616 | tf_op jit(solution)/shard_map/ppermute | solution.py:605

commit v3 on v2

--- a/solution.py
+++ b/solution.py
@@ -310,18 +310,17 @@
     for copy in copies:
         copy.wait()
 
-    def step(i, _):
+    def own_source(s):
+        kb = own[0][1, s] - my_row * blocks
+        return jnp.where((s < own[1][0]) & (kb >= 0) & (kb < blocks), kb, -1)
+
+    def step(i, seen):
         way, t = lax.div(i, SLOTS), lax.rem(i, SLOTS)
         kb = tags[jnp.minimum(way, len(got) - 1), 3, t].astype(jnp.int32) - my_row * blocks
         if own is not None:
-            pairs, count = own
-            before = jnp.int32(0)
-            for s in range(SLOTS + 1):
-                inside = (pairs[1, s] >= my_row * blocks) & (pairs[1, s] < (my_row + 1) * blocks)
-                before = before + jnp.where(inside & (s <= t), 1, 0)
-            left_over = (t + 1 < count[0]) & (before >= OWN_FIRST)
-            own_kb = jnp.where(left_over, pairs[1, t + 1] - my_row * blocks, -1)
-            kb = jnp.where(way == len(got), own_kb, kb)
+            own_kb = own_source(t + 1)
+            kb = jnp.where(way == len(got), jnp.where(seen >= OWN_FIRST, own_kb, -1), kb)
+            seen = seen + jnp.where((way == len(got)) & (own_kb >= 0), 1, 0)
 
         @pl.when((kb >= 0) & (kb < blocks))
         def _():
@@ -354,9 +353,10 @@
                 def _():
                     field[pl.ds(ka, 1), :] += cols * jnp.where(ka == kb, 0.0, 1.0)
 
-        return 0
-
-    lax.fori_loop(0, (len(got) + (own is not None)) * SLOTS, step, 0)
+        return seen
+
+    seen = jnp.int32(0) if own is None else jnp.where(own_source(0) >= 0, 1, 0)
+    lax.fori_loop(0, (len(got) + (own is not None)) * SLOTS, step, seen)
 
 
 def direct_kernel(pairs, count, near_ref, start, *refs, ways):

time: 50.3 us -> 53.5 us (1.064); the launches traced: 50.1 us -> 54.3 us
  starting transfers between devices: 24.7 us -> 28.7 us
    ppermute x3, starting transfers between devices: 3.43 us -> 10.3 us  [body(): lax.ppermute(both, 'col', [(i, (i - k) % n_col) for i in range(n_col)])]
    ppermute x7, starting transfers between devices: 15.1 us -> 13.4 us  [swap(): return lax.ppermute(x, axis, [(i, i ^ d) for i in range(n)])]
    ppermute x3, starting transfers between devices: 6.2 us -> 5.02 us  [body(): lax.ppermute(x, 'row', [(i, (i + k + 1) % n_row) for i in range(n_row)])]
  transfers between devices with their start and end apart: 13 -> 13, of which waited for: 5 -> 4; matrix products, arithmetic and copies ran while one was open for 0% -> 0% of each run, Pallas kernels for 17% -> 15%
where the time goes in v3:
time: 53.5 us; the launch traced here: 54.3 us
  starting transfers between devices  28.7 us (54%)
  Pallas kernels  12.2 us (23%)
  waiting for transfers between devices  11.9 us (22%)
  between operations  1.42 us (3%)
    ppermute x7, starting transfers between devices, swap(): return lax.ppermute(x, axis, [(i, i ^ d) for i in range(n)])  13.4 us
    ppermute x3, starting transfers between devices, body(): lax.ppermute(both, 'col', [(i, (i - k) % n_col) for i in range(n_col)])  10.3 us
    ppermute x7, waiting for transfers between devices, swap(): return lax.ppermute(x, axis, [(i, i ^ d) for i in range(n)])  9.98 us
    ppermute x3, starting transfers between devices, body(): lax.ppermute(x, 'row', [(i, (i + k + 1) % n_row) for i in range(n_row)])  5.02 us
    pallas_call x1, Pallas kernels, body(): pl.pallas_call(near_own_kernel, out_shape=f32(blocks, BLK), in_specs=[SME...  3.47 us
    pallas_call x1, Pallas kernels, body(): pl.pallas_call(functools.partial(far_kernel, direct=direct, base=base), o...  2.24 us
    ppermute x3, waiting for transfers between devices, body(): lax.ppermute(both, 'col', [(i, (i - k) % n_col) for i in range(n_col)])  1.91 us
    pallas_call x1, Pallas kernels, body(): pl.pallas_call(functools.partial(direct_kernel, ways=len(direct)), out_sh...  1.72 us
  transfers between devices with their start and end apart: 13, of which 4 were waited for; matrix products, arithmetic and copies ran while one was open for 0% of the time, Pallas kernels for 15%

profile of v3, /device:TPU:0, one launch (start us, length us, event | category | flops | bytes accessed | tf_op | source)
XLA Modules:
  0.0 54.3 jit_solution(17278765496609684448)
XLA Ops:
  0.7 1.4 %prep.1 = (f32[152,512]{1,0:T(8,128)S(1)}, f32[17,4,512]{2,1,0:T(4,128)S(1)}, f32[16,24,512]{2,1,0:T(8,128)S(1)}, f32[16,512]{1,0:T(8,128)S(1)}) custom-call(s32[2,6]{1,0:T(2,128)} %bitcast.7, s32[1]{0:T(128)S(6)} %copy.10.count, s32[2,16]{1,0:T(2,128)} %bitcast.4, f32[4,4,8192]{2,1,0:T(4,128)} %pts_hbm.1, f32[64,128]{1,0:T(8,128)} %bitcast.11), custom_call_target="tpu_custom_call" | custom-call | flops 1320000000 | bytes 65536 | tf_op jit(solution)/shard_map/prep/pallas_call | solution.py:505
  2.1 3.0 %collective-permute-start.2 = (f32[17,4,512]{2,1,0:T(4,128)S(1)}, f32[17,4,512]{2,1,0:T(4,128)S(1)}, u32[]{:S(2)}, u32[]{:S(2)}) collective-permute-start(f32[17,4,512]{2,1,0:T(4,128)S(1)} %get-tuple-element.25.own_in.own_far), channel_id=1, source_target_pairs={{0,4},{1,5},{2,6},{3,7},{4,0},{5,1},{6,2},{7,3},{8,12},{9,13},{10,... | collective-permute-start | bytes 417800 | tf_op jit(solution)/shard_map/ppermute | solution.py:488
  5.1 2.6 %collective-permute-start.1 = (f32[152,512]{1,0:T(8,128)S(1)}, f32[152,512]{1,0:T(8,128)S(1)}, u32[]{:S(2)}, u32[]{:S(2)}) collective-permute-start(f32[152,512]{1,0:T(8,128)S(1)} %get-tuple-element.24), channel_id=1, source_target_pairs={{0,16},{8,24},{16,0},{24,8},{1,17},{9,25},{17,1},{25,9},{2,18},{10... | collective-permute-start | bytes 933896 | tf_op jit(solution)/shard_map/ppermute | solution.py:488
  7.7 1.6 %collective-permute-start = (f32[152,512]{1,0:T(8,128)S(1)}, f32[152,512]{1,0:T(8,128)S(1)}, u32[]{:S(2)}, u32[]{:S(2)}) collective-permute-start(f32[152,512]{1,0:T(8,128)S(1)} %get-tuple-element.24), channel_id=1, source_target_pairs={{0,8},{8,0},{16,24},{24,16},{1,9},{9,1},{17,25},{25,17},{2,10},{10... | collective-permute-start | bytes 933896 | tf_op jit(solution)/shard_map/ppermute | solution.py:488
  9.3 0.0 collective-permute-done.2
  9.3 0.1 pad_maximum_fusion
  9.4 0.0 copy-start.1
  9.4 1.6 %collective-permute-start.3 = (f32[34,4,512]{2,1,0:T(4,128)S(1)}, f32[34,4,512]{2,1,0:T(4,128)S(1)}, u32[]{:S(2)}, u32[]{:S(2)}) collective-permute-start(f32[34,4,512]{2,1,0:T(4,128)S(1)} %pad_maximum_fusion), channel_id=1, source_target_pairs={{0,2},{1,3},{2,0},{3,1},{4,6},{5,7},{6,4},{7,5},{8,10},{9,11},{10,... | collective-permute-start | bytes 835592 | tf_op jit(solution)/shard_map/ppermute | solution.py:488
  10.9 0.0 copy-done.1
  10.9 3.5 %near_own.1.start = f32[16,512]{1,0:T(8,128)S(1)} custom-call(s32[2,6]{1,0:T(2,128)S(1)} %bitcast.8, s32[1]{0:T(128)S(6)} %copy.10.count, f32[16,24,512]{2,1,0:T(8,128)S(1)} %get-tuple-element.23.near_ref), custom_call_target="tpu_custom_call" | custom-call | flops 5500000256 | bytes 65536 | tf_op jit(solution)/shard_map/near_own/pallas_call | solution.py:542
  15.1 1.9 %collective-permute-done.3 = f32[34,4,512]{2,1,0:T(4,128)S(1)} collective-permute-done((f32[34,4,512]{2,1,0:T(4,128)S(1)}, f32[34,4,512]{2,1,0:T(4,128)S(1)}, u32[]{:S(2)}, u32[]{:S(2)}) %collective-permute-start.3) | collective-permute-done | bytes 278560 | tf_op jit(solution)/shard_map/ppermute | solution.py:488
  17.0 0.0 copy-start
  17.0 0.1 collective-permute-start.4
  17.1 4.5 %collective-permute-done.1.refs_1_ = f32[152,512]{1,0:T(8,128)S(1)} collective-permute-done((f32[152,512]{1,0:T(8,128)S(1)}, f32[152,512]{1,0:T(8,128)S(1)}, u32[]{:S(2)}, u32[]{:S(2)}) %collective-permute-start.1) | collective-permute-done | bytes 311328 | tf_op jit(solution)/shard_map/ppermute | solution.py:488
  21.6 0.6 %collective-permute-start.5 = (f32[152,512]{1,0:T(8,128)S(1)}, f32[152,512]{1,0:T(8,128)S(1)}, u32[]{:S(2)}, u32[]{:S(2)}) collective-permute-start(f32[152,512]{1,0:T(8,128)S(1)} %collective-permute-done.1.refs_1_), channel_id=1, source_target_pairs={{0,8},{8,0},{16,24},{24,16},{1,9},{9,1},{17,25},{25,17},{2,10},{10... | collective-permute-start | bytes 933896 | tf_op jit(solution)/shard_map/ppermute | solution.py:488
  22.2 0.0 collective-permute-done.refs_0_
  22.2 1.7 %near_direct.1 = (f32[16,512]{1,0:T(8,128)S(1)}, f32[8,512]{1,0:T(8,128)S(1)}, f32[8,512]{1,0:T(8,128)S(1)}) custom-call(s32[2,6]{1,0:T(2,128)S(1)} %bitcast.9, s32[1]{0:T(128)S(6)} %copy.10.count, f32[16,24,512]{2,1,0:T(8,128)S(1)} %get-tuple-element.23.near_ref, f32[16,512]{1,0:T(8,128)S(1)} %near_own.1.start, ...), custom_call_target="tpu_custom_call" | custom-call | flops 32999999488 | bytes 65536 | tf_op jit(solution)/shard_map/near_direct/pallas_call | solution.py:568
  23.9 0.0 collective-permute-done.4.row1
  23.9 0.0 copy-done
  23.9 2.2 %far_direct.1 = (f32[16,512]{1,0:T(8,128)S(1)}, f32[16,512]{1,0:T(8,128)S(1)}) custom-call(s32[2,16]{1,0:T(2,128)S(1)} %bitcast.5, s32[1]{0:T(128)S(6)} %copy.11.count, f32[68,4,512]{2,1,0:T(4,128)S(1)} %constant_dynamic-update-slice_fusion.row0, f32[68,4,512]{2,1,0:T(4,128)S(1)} %collective-permute-done.4.row1, ...), custom_call_target="tpu_custom_call" | custom-call | flops 3300000000 | bytes 65536 | tf_op jit(solution)/shard_map/far_direct/pallas_call | solution.py:578
  26.2 3.6 %collective-permute-done.5.refs_0_.refs_2_ = f32[152,512]{1,0:T(8,128)S(1)} collective-permute-done((f32[152,512]{1,0:T(8,128)S(1)}, f32[152,512]{1,0:T(8,128)S(1)}, u32[]{:S(2)}, u32[]{:S(2)}) %collective-permute-start.5) | collective-permute-done | bytes 311328 | tf_op jit(solution)/shard_map/ppermute | solution.py:488
  29.8 1.6 %late.1 = (f32[16,512]{1,0:T(8,128)S(1)}, f32[16,512]{1,0:T(8,128)S(1)}, f32[16,512]{1,0:T(8,128)S(1)}, f32[24,512]{1,0:T(8,128)S(1)}, f32[24,512]{1,0:T(8,128)S(1)}, /*index=5*/f32[24,512]{1,0:T(8,128)S(1)}) custom-call(s32[2,16]{1,0:T(2,128)S(1)} %bitcast.6, s32[1]{0:T(128)S(6)} %copy.11.count, f32[16,24,512]{2,1,0:T(8,128)S(1)} %get-tuple-element.23.near_ref, ...), custom_call_target="tpu_custom_call" | custom-call | flops 8800000000 | bytes 65536 | tf_op jit(solution)/shard_map/late/pallas_call | solution.py:588
  31.4 4.0 %collective-permute-start.9 = (f32[16,512]{1,0:T(8,128)S(1)}, f32[16,512]{1,0:T(8,128)S(1)}, u32[]{:S(2)}, u32[]{:S(2)}) collective-permute-start(f32[16,512]{1,0:T(8,128)S(1)} %get-tuple-element.38), channel_id=1, source_target_pairs={{0,1},{1,0},{2,3},{3,2},{4,5},{5,4},{6,7},{7,6},{8,9},{9,8},{10,11... | collective-permute-start | bytes 98312 | tf_op jit(solution)/shard_map/ppermute | solution.py:488
  35.4 0.8 %collective-permute-start.6 = (f32[24,512]{1,0:T(8,128)S(1)}, f32[24,512]{1,0:T(8,128)S(1)}, u32[]{:S(2)}, u32[]{:S(2)}) collective-permute-start(f32[24,512]{1,0:T(8,128)S(1)} %get-tuple-element.35), channel_id=1, source_target_pairs={{0,8},{8,16},{16,24},{24,0},{1,9},{9,17},{17,25},{25,1},{2,10},{10... | collective-permute-start | bytes 147464 | tf_op jit(solution)/shard_map/ppermute | solution.py:600
  36.2 2.6 %collective-permute-start.7 = (f32[24,512]{1,0:T(8,128)S(1)}, f32[24,512]{1,0:T(8,128)S(1)}, u32[]{:S(2)}, u32[]{:S(2)}) collective-permute-start(f32[24,512]{1,0:T(8,128)S(1)} %get-tuple-element.36), channel_id=1, source_target_pairs={{0,16},{8,24},{16,0},{24,8},{1,17},{9,25},{17,1},{25,9},{2,18},{10... | collective-permute-start | bytes 147464 | tf_op jit(solution)/shard_map/ppermute | solution.py:600
  38.8 1.6 %collective-permute-start.8 = (f32[24,512]{1,0:T(8,128)S(1)}, f32[24,512]{1,0:T(8,128)S(1)}, u32[]{:S(2)}, u32[]{:S(2)}) collective-permute-start(f32[24,512]{1,0:T(8,128)S(1)} %get-tuple-element.37), channel_id=1, source_target_pairs={{0,24},{8,0},{16,8},{24,16},{1,25},{9,1},{17,9},{25,17},{2,26},{10... | collective-permute-start | bytes 147464 | tf_op jit(solution)/shard_map/ppermute | solution.py:600
  40.4 0.0 collective-permute-done.9
  40.4 8.8 %collective-permute-start.12 = (f32[32,512]{1,0:T(8,128)S(1)}, f32[32,512]{1,0:T(8,128)S(1)}, u32[]{:S(2)}, u32[]{:S(2)}) collective-permute-start(f32[32,512]{1,0:T(8,128)S(1)} %constant_dynamic-update-slice_fusion.3.refs_0_), channel_id=1, source_target_pairs={{0,2},{1,3},{2,4},{3,5},{4,6},{5,7},{6,0},{7,1},{8,10},{9,11},{10,... | collective-permute-start | bytes 196616 | tf_op jit(solution)/shard_map/ppermute | solution.py:605
  49.2 0.0 collective-permute-start.11
  49.2 0.0 collective-permute-done.6.refs_3_
  49.2 1.5 %collective-permute-start.10 = (f32[32,512]{1,0:T(8,128)S(1)}, f32[32,512]{1,0:T(8,128)S(1)}, u32[]{:S(2)}, u32[]{:S(2)}) collective-permute-start(f32[32,512]{1,0:T(8,128)S(1)} %constant_dynamic-update-slice_fusion.3.refs_0_), channel_id=1, source_target_pairs={{0,6},{1,7},{2,0},{3,1},{4,2},{5,3},{6,4},{7,5},{8,14},{9,15},{10,... | collective-permute-start | bytes 196616 | tf_op jit(solution)/shard_map/ppermute | solution.py:605
  50.7 0.0 collective-permute-done.7.refs_4_
  50.7 0.0 collective-permute-done.8.refs_5_
  50.7 0.8 %final_cols.1.field = f32[16,512]{1,0:T(8,128)S(1)} custom-call(s32[2,6]{1,0:T(2,128)S(1)} %bitcast.10, f32[16,512]{1,0:T(8,128)S(1)} %get-tuple-element.22.weight, f32[16,512]{1,0:T(8,128)S(1)} %get-tuple-element.33.near, f32[17,4,512]{2,1,0:T(4,128)S(1)} %get-tuple-element.25.own_in.own_far, f32[16,512]{1,0:T(8,128)S(1)} %get-tuple-element.34.own_cols, ...), custom_call_target="tpu_custom_call" | custom-call | flops 1100000000 | bytes 65536 | tf_op jit(solution)/shard_map/final_cols/pallas_call | solution.py:606
  51.6 0.0 collective-permute-done.12.refs_3_
  51.6 1.9 %collective-permute-done.11.refs_2_ = f32[32,512]{1,0:T(8,128)S(1)} collective-permute-done((f32[32,512]{1,0:T(8,128)S(1)}, f32[32,512]{1,0:T(8,128)S(1)}, u32[]{:S(2)}, u32[]{:S(2)}) %collective-permute-start.11) | collective-permute-done | bytes 65568 | tf_op jit(solution)/shard_map/ppermute | solution.py:605
  53.5 0.0 collective-permute-done.10.refs_1_
  53.5 0.9 %final_rows.1 = f32[64,128]{1,0:T(8,128)} custom-call(f32[16,512]{1,0:T(8,128)S(1)} %get-tuple-element.22.weight, f32[16,512]{1,0:T(8,128)S(1)} %final_cols.1.field, f32[68,4,512]{2,1,0:T(4,128)S(1)} %constant_dynamic-update-slice_fusion.row0, f32[68,4,512]{2,1,0:T(4,128)S(1)} %collective-permute-done.4.row1, ...), custom_call_target="tpu_custom_call" | custom-call | flops 1100000000 | bytes 65536 | tf_op jit(solution)/shard_map/final_rows/pallas_call | solution.py:615
  (5 shorter events, 0.1 us)
Async XLA Ops:
  2.1 7.2 %collective-permute-start.2 = (f32[17,4,512]{2,1,0:T(4,128)S(1)}, f32[17,4,512]{2,1,0:T(4,128)S(1)}, u32[]{:S(2)}, u32[]{:S(2)}) collective-permute-start(f32[17,4,512]{2,1,0:T(4,128)S(1)} %get-tuple-element.25.own_in.own_far), channel_id=1, source_target_pairs={{0,4},{1,5},{2,6},{3,7},{4,0},{5,1},{6,2},{7,3},{8,12},{9,13},{10,... | collective-permute-start | bytes 417800 | tf_op jit(solution)/shard_map/ppermute | solution.py:488
  5.1 16.5 %collective-permute-start.1 = (f32[152,512]{1,0:T(8,128)S(1)}, f32[152,512]{1,0:T(8,128)S(1)}, u32[]{:S(2)}, u32[]{:S(2)}) collective-permute-start(f32[152,512]{1,0:T(8,128)S(1)} %get-tuple-element.24), channel_id=1, source_target_pairs={{0,16},{8,24},{16,0},{24,8},{1,17},{9,25},{17,1},{25,9},{2,18},{10... | collective-permute-start | bytes 933896 | tf_op jit(solution)/shard_map/ppermute | solution.py:488
  7.7 14.5 %collective-permute-start = (f32[152,512]{1,0:T(8,128)S(1)}, f32[152,512]{1,0:T(8,128)S(1)}, u32[]{:S(2)}, u32[]{:S(2)}) collective-permute-start(f32[152,512]{1,0:T(8,128)S(1)} %get-tuple-element.24), channel_id=1, source_target_pairs={{0,8},{8,0},{16,24},{24,16},{1,9},{9,1},{17,25},{25,17},{2,10},{10... | collective-permute-start | bytes 933896 | tf_op jit(solution)/shard_map/ppermute | solution.py:488
  9.4 1.6 %copy-start.1 = (s32[6,2]{0,1:T(2,128)S(1)}, s32[6,2]{0,1:T(2,128)}, u32[]{:S(2)}) copy-start(s32[6,2]{0,1:T(2,128)} %param.8) | copy-start | bytes 148
  9.4 7.6 %collective-permute-start.3 = (f32[34,4,512]{2,1,0:T(4,128)S(1)}, f32[34,4,512]{2,1,0:T(4,128)S(1)}, u32[]{:S(2)}, u32[]{:S(2)}) collective-permute-start(f32[34,4,512]{2,1,0:T(4,128)S(1)} %pad_maximum_fusion), channel_id=1, source_target_pairs={{0,2},{1,3},{2,0},{3,1},{4,6},{5,7},{6,4},{7,5},{8,10},{9,11},{10,... | collective-permute-start | bytes 835592 | tf_op jit(solution)/shard_map/ppermute | solution.py:488
  17.0 6.9 %copy-start = (s32[16,2]{0,1:T(2,128)S(1)}, s32[16,2]{0,1:T(2,128)}, u32[]{:S(2)}) copy-start(s32[16,2]{0,1:T(2,128)} %param.9) | copy-start | bytes 388
  17.0 6.9 %collective-permute-start.4 = (f32[68,4,512]{2,1,0:T(4,128)S(1)}, f32[68,4,512]{2,1,0:T(4,128)S(1)}, u32[]{:S(2)}, u32[]{:S(2)}) collective-permute-start(f32[68,4,512]{2,1,0:T(4,128)S(1)} %constant_dynamic-update-slice_fusion.row0), channel_id=1, source_target_pairs={{0,1},{1,0},{2,3},{3,2},{4,5},{5,4},{6,7},{7,6},{8,9},{9,8},{10,11... | collective-permute-start | bytes 1671176 | tf_op jit(solution)/shard_map/ppermute | solution.py:488
  21.6 8.1 %collective-permute-start.5 = (f32[152,512]{1,0:T(8,128)S(1)}, f32[152,512]{1,0:T(8,128)S(1)}, u32[]{:S(2)}, u32[]{:S(2)}) collective-permute-start(f32[152,512]{1,0:T(8,128)S(1)} %collective-permute-done.1.refs_1_), channel_id=1, source_target_pairs={{0,8},{8,0},{16,24},{24,16},{1,9},{9,1},{17,25},{25,17},{2,10},{10... | collective-permute-start | bytes 933896 | tf_op jit(solution)/shard_map/ppermute | solution.py:488
  31.4 9.0 %collective-permute-start.9 = (f32[16,512]{1,0:T(8,128)S(1)}, f32[16,512]{1,0:T(8,128)S(1)}, u32[]{:S(2)}, u32[]{:S(2)}) collective-permute-start(f32[16,512]{1,0:T(8,128)S(1)} %get-tuple-element.38), channel_id=1, source_target_pairs={{0,1},{1,0},{2,3},{3,2},{4,5},{5,4},{6,7},{7,6},{8,9},{9,8},{10,11... | collective-permute-start | bytes 98312 | tf_op jit(solution)/shard_map/ppermute | solution.py:488
  35.4 13.8 %collective-permute-start.6 = (f32[24,512]{1,0:T(8,128)S(1)}, f32[24,512]{1,0:T(8,128)S(1)}, u32[]{:S(2)}, u32[]{:S(2)}) collective-permute-start(f32[24,512]{1,0:T(8,128)S(1)} %get-tuple-element.35), channel_id=1, source_target_pairs={{0,8},{8,16},{16,24},{24,0},{1,9},{9,17},{17,25},{25,1},{2,10},{10... | collective-permute-start | bytes 147464 | tf_op jit(solution)/shard_map/ppermute | solution.py:600
  36.2 14.6 %collective-permute-start.7 = (f32[24,512]{1,0:T(8,128)S(1)}, f32[24,512]{1,0:T(8,128)S(1)}, u32[]{:S(2)}, u32[]{:S(2)}) collective-permute-start(f32[24,512]{1,0:T(8,128)S(1)} %get-tuple-element.36), channel_id=1, source_target_pairs={{0,16},{8,24},{16,0},{24,8},{1,17},{9,25},{17,1},{25,9},{2,18},{10... | collective-permute-start | bytes 147464 | tf_op jit(solution)/shard_map/ppermute | solution.py:600
  38.8 12.0 %collective-permute-start.8 = (f32[24,512]{1,0:T(8,128)S(1)}, f32[24,512]{1,0:T(8,128)S(1)}, u32[]{:S(2)}, u32[]{:S(2)}) collective-permute-start(f32[24,512]{1,0:T(8,128)S(1)} %get-tuple-element.37), channel_id=1, source_target_pairs={{0,24},{8,0},{16,8},{24,16},{1,25},{9,1},{17,9},{25,17},{2,26},{10... | collective-permute-start | bytes 147464 | tf_op jit(solution)/shard_map/ppermute | solution.py:600
  40.4 11.2 %collective-permute-start.12 = (f32[32,512]{1,0:T(8,128)S(1)}, f32[32,512]{1,0:T(8,128)S(1)}, u32[]{:S(2)}, u32[]{:S(2)}) collective-permute-start(f32[32,512]{1,0:T(8,128)S(1)} %constant_dynamic-update-slice_fusion.3.refs_0_), channel_id=1, source_target_pairs={{0,2},{1,3},{2,4},{3,5},{4,6},{5,7},{6,0},{7,1},{8,10},{9,11},{10,... | collective-permute-start | bytes 196616 | tf_op jit(solution)/shard_map/ppermute | solution.py:605
  49.2 4.3 %collective-permute-start.11 = (f32[32,512]{1,0:T(8,128)S(1)}, f32[32,512]{1,0:T(8,128)S(1)}, u32[]{:S(2)}, u32[]{:S(2)}) collective-permute-start(f32[32,512]{1,0:T(8,128)S(1)} %constant_dynamic-update-slice_fusion.3.refs_0_), channel_id=1, source_target_pairs={{0,4},{1,5},{2,6},{3,7},{4,0},{5,1},{6,2},{7,3},{8,12},{9,13},{10,... | collective-permute-start | bytes 196616 | tf_op jit(solution)/shard_map/ppermute | solution.py:605
  49.2 4.3 %collective-permute-start.10 = (f32[32,512]{1,0:T(8,128)S(1)}, f32[32,512]{1,0:T(8,128)S(1)}, u32[]{:S(2)}, u32[]{:S(2)}) collective-permute-start(f32[32,512]{1,0:T(8,128)S(1)} %constant_dynamic-update-slice_fusion.3.refs_0_), channel_id=1, source_target_pairs={{0,6},{1,7},{2,0},{3,1},{4,2},{5,3},{6,4},{7,5},{8,14},{9,15},{10,... | collective-permute-start | bytes 196616 | tf_op jit(solution)/shard_map/ppermute | solution.py:605
